TPU v7x, 32 devices: a whole 2x2x4 slice. The times are simulated.
32 devices in a mesh: groups: 2 (over x), facet: 16 (over z, y, core).
Axes of the slice: x: 2, y: 2, z: 4, core: 2. Of those that a mesh axis runs over, the one named last changes fastest.
Arguments:
- visibility: bfloat16 [16384, 128], P(('groups', 'facet')), parts along dimension 0, may hold values from -6 to 6
- facet_of: int32 [16384, 1], P(('groups', 'facet')), parts along dimension 0, may hold values from 0 to 15; in each aligned block of 512 rows (0 to 511, 512 to 1023, ...) at most 64 rows name the same one
- cell_of: int32 [16384], P(('groups', 'facet')), parts along dimension 0, may hold values from 0 to 16383
- taper: bfloat16 [32768, 128], P(('groups', 'facet')), parts along dimension 0, may hold values from -1 to 1
- model: bfloat16 [524288, 128], P(('groups', 'facet')), parts along dimension 0, may hold values from -6 to 6
Outputs:
- model_next: bfloat16 [524288, 128], P(('groups', 'facet')), parts along dimension 0
- residual: bfloat16 [16384, 128], P(('groups', 'facet')), parts along dimension 0
There are 2 independent parts, one for each index of `groups`. A program takes and returns all parts, laid end to end along the dimension named above; each array names one. Nothing has to cross between parts.
Inputs may be any that keep to these rules, and one draw needn't show every extreme that they name: `facet_of`: every facet is named by some row; at most 64 rows of one device name one facet, and in every draw some device has exactly 64 rows for one facet.
All inputs are finite; a program needn't handle non-finite values.
Results may differ from a plain program's by a relative error of at most 0.0058.
Values may be sent and summed in bfloat16 or wider, within the bound.
A program may use at most 128 MiB of HBM per device.

v0:
```python
import math

import jax
import jax.numpy as jnp
from jax import lax
from jax.sharding import PartitionSpec as P

GU = 128
GV = 128
CELLS = 16384


loop_gain = 0.1


def complex_product(left, right):
    midway = left.shape[-1] // 2
    left_real, left_imaginary = (left[..., :midway], left[..., midway:])
    right_real, right_imaginary = (right[..., :midway], right[..., midway:])
    return jnp.concatenate(
        [
            left_real * right_real - left_imaginary * right_imaginary,
            left_real * right_imaginary + left_imaginary * right_real,
        ],
        -1,
    )


def conjugate(values):
    midway = values.shape[-1] // 2
    return jnp.concatenate([values[..., :midway], -values[..., midway:]], -1)


def dft_table(length, orient):
    ordinal = jnp.arange(length, dtype=jnp.int32)
    phases = ordinal[:, None] * ordinal[None, :] % length
    angles = phases.astype(jnp.float32) * (2.0 * math.pi / length)
    return jnp.concatenate([jnp.cos(angles), orient * jnp.sin(angles)], 0).astype(jnp.bfloat16)


def along_axis(volume, length, orient, pattern, axis):
    table = dft_table(length, orient)
    stacked = jnp.einsum(pattern, table, volume, preferred_element_type=jnp.float32)
    leading = lax.slice_in_dim(stacked, 0, length, axis=axis)
    second = lax.slice_in_dim(stacked, length, 2 * length, axis=axis)
    midway = volume.shape[-1] // 2
    joined = jnp.concatenate(
        [
            leading[..., :midway] - second[..., midway:],
            leading[..., midway:] + second[..., :midway],
        ],
        -1,
    )
    return joined.astype(jnp.bfloat16)


def transform(plane, orient, extent_u, extent_v):
    columns = plane.shape[-1]
    volume = plane.reshape(extent_u, extent_v, columns)
    volume = along_axis(volume, extent_u, orient, "pu,uvc->pvc", 0)
    volume = along_axis(volume, extent_v, orient, "qv,pvc->pqc", 1)
    return volume.reshape(extent_u * extent_v, columns)


def body(visibility, facet_of, cell_of, taper, model):
    peer_count = lax.axis_size("facet")
    local_rows = visibility.shape[0]
    capacity = 2 * local_rows // peer_count
    columns = visibility.shape[1]
    target = facet_of[:, 0]
    choose = (target[:, None] == jnp.arange(peer_count, dtype=jnp.int32)[None, :]).astype(jnp.int32)
    before = jnp.cumsum(choose, axis=0) - choose
    position = target * capacity + jnp.sum(before * choose, axis=1)
    send_rows = (
        jnp.zeros((peer_count * capacity, columns), jnp.bfloat16).at[position].set(visibility)
    )
    send_cells = jnp.full((peer_count * capacity,), CELLS, jnp.int32).at[position].set(cell_of)
    slot_rows, cell_ids = (
        lax.all_to_all(
            send_rows.reshape(peer_count, capacity, columns),
            "facet",
            split_axis=0,
            concat_axis=0,
            tiled=True,
        ),
        lax.all_to_all(
            send_cells.reshape(peer_count, capacity),
            "facet",
            split_axis=0,
            concat_axis=0,
            tiled=True,
        ),
    )
    slot_rows = slot_rows.reshape(peer_count * capacity, columns)
    cell_ids = cell_ids.reshape(peer_count * capacity)
    row_count = jnp.sum((cell_ids < CELLS).astype(jnp.float32))
    slot_wide = slot_rows.astype(jnp.float32)
    grid_sum = jax.ops.segment_sum(slot_wide, cell_ids, num_segments=CELLS + 1)[:CELLS]
    panel_all = lax.all_gather(taper, "facet", axis=0, tiled=True).astype(jnp.float32)
    tapered = complex_product(grid_sum, panel_all).astype(jnp.bfloat16)
    dirty_image = transform(tapered, -1, GU, GV).astype(jnp.float32) / jnp.sqrt(row_count)
    model_sum = model.astype(jnp.float32) + loop_gain * dirty_image
    model_next = model_sum.astype(jnp.bfloat16)
    spectrum = transform(model_next, 1, GU, GV).astype(jnp.float32) / math.sqrt(CELLS)
    degrid_panel = lax.all_gather(taper, "facet", axis=0, tiled=True).astype(jnp.float32)
    model_grid = complex_product(spectrum, conjugate(degrid_panel))
    predicted = jnp.take(model_grid, jnp.minimum(cell_ids, CELLS - 1), axis=0)
    answer = (slot_wide - predicted).astype(jnp.bfloat16)
    returned = lax.all_to_all(
        answer.reshape(peer_count, capacity, columns),
        "facet",
        split_axis=0,
        concat_axis=0,
        tiled=True,
    )
    residual = returned.reshape(peer_count * capacity, columns)[position]
    return (model_next, residual)


def solution(mesh):
    placed = (
        P(("groups", "facet"), None),
        P(("groups", "facet"), None),
        P(("groups", "facet")),
        P(("groups", "facet"), None),
        P(("groups", "facet"), None),
    )
    return jax.shard_map(
        body,
        mesh=mesh,
        in_specs=placed,
        out_specs=(P(("groups", "facet"), None), P(("groups", "facet"), None)),
        check_vma=False,
    )
```

profile of v0, /device:TPU:1, one launch (start us, length us, event | category | flops | bytes accessed | tf_op | source)
XLA Modules:
  0.0 225.4 jit_solution(5947595093684710682)
XLA Ops:
  14.7 7.3 %all-to-all-start = ((s32[16,1,64]{2,1,0:T(1,128)}), s32[16,1,64]{2,1,0:T(1,128)S(1)}, u32[]{:S(2)}, u32[]{:S(2)}) async-start(s32[16,1,64]{2,1,0:T(1,128)} %all_to_all.12), calls=%async_computation | async-start | bytes 16384 | tf_op jit(solution)/shard_map/all_to_all | solution.py:86
  22.6 6.4 %copy.26 = bf16[16384,128]{0,1:T(8,128)(2,1)} copy(bf16[16384,128]{1,0:T(8,128)(2,1)} %param.9) | data formatting | bytes 8388608 | tf_op args[4]
  31.8 6.0 %all-to-all-start.1 = ((bf16[16,64,128]{2,1,0:T(8,128)(2,1)}), bf16[16,64,128]{2,1,0:T(8,128)(2,1)S(1)}, u32[]{:S(2)}, u32[]{:S(2)}) async-start(bf16[16,64,128]{2,1,0:T(8,128)(2,1)} %bitcast.5), calls=%async_computation.1 | async-start | bytes 524288 | tf_op jit(solution)/shard_map/all_to_all | solution.py:79
  40.5 10.2 %all-to-all-done.1 = bf16[16,64,128]{2,1,0:T(8,128)(2,1)S(1)} async-done(((bf16[16,64,128]{2,1,0:T(8,128)(2,1)}), bf16[16,64,128]{2,1,0:T(8,128)(2,1)S(1)}, u32[]{:S(2)}, u32[]{:S(2)}) %all-to-all-start.1) | async-done | bytes 262176 | tf_op jit(solution)/shard_map/all_to_all | solution.py:79
  50.6 9.8 %scatter_custom_fusion.2 = f32[16385,128]{1,0:T(8,128)} fusion(s32[1024]{0:T(1024)S(1)} %reshape.132, f32[]{:T(128)} %constant.56.clone.1, bf16[1024,128]{1,0:T(8,128)(2,1)S(1)} %bitcast.81), kind=kCustom, calls=%fused_computation.14 | custom fusion | flops 262144 | bytes 8651268 | tf_op jit(solution)/shard_map/scatter-add | solution.py:98
  60.4 5.4 %all-gather.2.cloned.1.call-done = bf16[16384,128]{1,0:T(8,128)(2,1)} async-done(((bf16[1024,128]{1,0:T(8,128)(2,1)}), bf16[16384,128]{1,0:T(8,128)(2,1)}) %all-gather.2.cloned.1.call-update) | async-done | bytes 4194320 | tf_op jit(solution)/shard_map/all_gather | solution.py:99
  68.4 13.0 %subtract_convert_fusion = (bf16[16384,64]{1,0:T(8,128)(2,1)}, bf16[16384,64]{1,0:T(8,128)(2,1)}) fusion(f32[16385,128]{1,0:T(8,128)} %scatter_custom_fusion.2, f32[16384,128]{1,0:T(8,128)S(1)} %convert_element_type.71), kind=kLoop, calls=%fused_computation.13 | loop fusion | flops 8388608 | bytes 20971520 | tf_op jit(solution)/shard_map/convert.18
  81.4 5.6 %copy.30 = bf16[128,128,64]{0,2,1:T(8,128)(2,1)S(1)} copy(bf16[128,128,64]{2,1,0:T(8,128)(2,1)} %bitcast.74) | data formatting | bytes 4194304 | tf_op jit(solution)/shard_map/concatenate | solution.py:20
  87.0 6.5 %copy.31 = bf16[128,128,64]{0,2,1:T(8,128)(2,1)} copy(bf16[128,128,64]{2,1,0:T(8,128)(2,1)} %bitcast.73) | data formatting | bytes 4194304 | tf_op jit(solution)/shard_map/concatenate | solution.py:20
  102.1 7.3 %copy.32 = bf16[128,128,128]{1,2,0:T(8,128)(2,1)} copy(bf16[128,128,128]{0,2,1:T(8,128)(2,1)} %pad_maximum_fusion.2) | data formatting | bytes 8388608 | tf_op jit(solution)/shard_map/concatenate | solution.py:47
  109.4 4.5 %convolution_bitcast_fusion.1 = f32[128,256,128]{1,2,0:T(8,128)S(1)} fusion(bf16[128,128,128]{1,2,0:T(8,128)(2,1)} %copy.32, bf16[128,128]{1,0:T(8,128)(2,1)S(1)} %get-tuple-element.22, bf16[128,128]{1,0:T(8,128)(2,1)S(1)} %get-tuple-element.21), kind=kOutput, calls=%fused_computation.6 | convolution fusion | flops 1073872896 | bytes 21037056 | tf_op jit(solution)/shard_map/qv,pvc->pqc/dot_general | solution.py:43
  119.8 3.4 %copy.53 = bf16[16,8,128,128]{3,2,1,0:T(8,128)(2,1)} copy(bf16[16,8,128,128]{3,1,2,0:T(8,128)(2,1)S(1)} %bitcast.70) | data formatting | bytes 8388608
  123.2 6.7 %copy.35 = bf16[128,128,128]{0,2,1:T(8,128)(2,1)} copy(bf16[128,128,128]{1,0,2:T(8,128)(2,1)} %bitcast.75) | data formatting | bytes 8388608 | tf_op jit(solution)/shard_map/reshape | solution.py:59
  129.9 4.5 %fusion.23 = f32[256,16384]{0,1:S(1)} fusion(bf16[128,16384]{0,1:T(8,128)(2,1)} %bitcast.72, bf16[128,128]{1,0:T(8,128)(2,1)S(1)} %get-tuple-element.22, bf16[128,128]{1,0:T(8,128)(2,1)S(1)} %fusion.28), kind=kOutput, calls=%fused_computation.58 | convolution fusion | flops 1073872896 | bytes 21037056
  138.7 7.3 %copy.36 = bf16[128,128,128]{1,2,0:T(8,128)(2,1)} copy(bf16[128,128,128]{0,2,1:T(8,128)(2,1)} %pad_maximum_fusion.3) | data formatting | bytes 8388608 | tf_op jit(solution)/shard_map/concatenate | solution.py:47
  146.0 4.5 %convolution_bitcast_fusion = f32[128,256,128]{1,2,0:T(8,128)S(1)} fusion(bf16[128,128,128]{1,2,0:T(8,128)(2,1)} %copy.36, bf16[128,128]{1,0:T(8,128)(2,1)S(1)} %get-tuple-element.22, bf16[128,128]{1,0:T(8,128)(2,1)S(1)} %fusion.28), kind=kOutput, calls=%fused_computation.5 | convolution fusion | flops 1073872896 | bytes 21037056 | tf_op jit(solution)/shard_map/qv,pvc->pqc/dot_general | solution.py:43
  153.5 4.8 %copy.46 = bf16[128,128,64]{2,1,0:T(8,128)(2,1)} copy(bf16[128,128,64]{1,2,0:T(8,128)(2,1)} %get-tuple-element.12) | data formatting | bytes 4194304 | tf_op jit(solution)/shard_map/concatenate | solution.py:47
  161.3 6.6 %convert_multiply_fusion = f32[16384,128]{1,0:T(8,128)} fusion(bf16[16384,64]{1,0:T(8,128)(2,1)} %bitcast.77, bf16[16384,64]{1,0:T(8,128)(2,1)} %bitcast.76), kind=kLoop, calls=%fused_computation.10 | loop fusion | flops 10485760 | bytes 12582912 | tf_op jit(solution)/shard_map/div | solution.py:104
  167.9 18.7 %multiply_subtract_fusion = (f32[16384,64]{1,0:T(8,128)}, f32[16384,64]{1,0:T(8,128)}) fusion(f32[16384,128]{1,0:T(8,128)} %convert_multiply_fusion, f32[16384,128]{1,0:T(8,128)} %copy-done), kind=kLoop, calls=%fused_computation.9 | loop fusion | flops 7340032 | bytes 25165824 | tf_op jit(solution)/shard_map/sub | solution.py:22
  186.6 9.5 %pad_maximum_fusion = f32[16384,128]{1,0:T(8,128)} fusion(f32[16384,64]{1,0:T(8,128)} %get-tuple-element.11, f32[16384,64]{1,0:T(8,128)} %get-tuple-element.10), kind=kLoop, calls=%fused_computation.7 | loop fusion | flops 2097152 | bytes 16777216 | tf_op jit(solution)/shard_map/concatenate | solution.py:20
  196.1 6.2 %gather_fusion = f32[1024,128]{1,0:T(8,128)S(1)} fusion(f32[16384,128]{1,0:T(8,128)} %pad_maximum_fusion, s32[1024]{0:T(1024)S(1)} %broadcast_clamp_fusion), kind=kCustom, calls=%fused_computation | custom fusion | bytes 1052672 | tf_op jit(solution)/shard_map/jit(_take)/gather | solution.py:107
  203.2 4.0 %all-to-all-start.2 = ((bf16[16,64,128]{2,1,0:T(8,128)(2,1)}), bf16[16,64,128]{2,1,0:T(8,128)(2,1)S(1)}, u32[]{:S(2)}, u32[]{:S(2)}) async-start(bf16[16,64,128]{2,1,0:T(8,128)(2,1)} %subtract_convert_fusion.1), calls=%async_computation.2 | async-start | bytes 524288 | tf_op jit(solution)/shard_map/all_to_all | solution.py:109
  207.2 6.4 %copy.41 = bf16[16384,128]{1,0:T(8,128)(2,1)} copy(bf16[16384,128]{0,1:T(8,128)(2,1)} %copy-done.1) | data formatting | bytes 8388608
  213.6 3.1 %all-to-all-done.2 = bf16[16,64,128]{2,1,0:T(8,128)(2,1)S(1)} async-done(((bf16[16,64,128]{2,1,0:T(8,128)(2,1)}), bf16[16,64,128]{2,1,0:T(8,128)(2,1)S(1)}, u32[]{:S(2)}, u32[]{:S(2)}) %all-to-all-start.2) | async-done | bytes 262176 | tf_op jit(solution)/shard_map/all_to_all | solution.py:109
  (45 shorter events, 42.9 us)
Async XLA Ops:
  7.2 58.7 %all-gather.2.cloned.1.call-start = ((), (), s32[]{:S(2)}) async-start(), calls=%async_computation.3 | async-start | bytes 4456448 | tf_op jit(solution)/shard_map/all_gather | solution.py:99
  14.7 17.0 %all-to-all-start = ((s32[16,1,64]{2,1,0:T(1,128)}), s32[16,1,64]{2,1,0:T(1,128)S(1)}, u32[]{:S(2)}, u32[]{:S(2)}) async-start(s32[16,1,64]{2,1,0:T(1,128)} %all_to_all.12), calls=%async_computation | async-start | bytes 16384 | tf_op jit(solution)/shard_map/all_to_all | solution.py:86
  31.8 18.9 %all-to-all-start.1 = ((bf16[16,64,128]{2,1,0:T(8,128)(2,1)}), bf16[16,64,128]{2,1,0:T(8,128)(2,1)S(1)}, u32[]{:S(2)}, u32[]{:S(2)}) async-start(bf16[16,64,128]{2,1,0:T(8,128)(2,1)} %bitcast.5), calls=%async_computation.1 | async-start | bytes 524288 | tf_op jit(solution)/shard_map/all_to_all | solution.py:79
  68.4 13.0 %copy-start = (f32[16384,128]{1,0:T(8,128)}, f32[16384,128]{1,0:T(8,128)S(1)}, u32[]{:S(2)}) copy-start(f32[16384,128]{1,0:T(8,128)S(1)} %convert_element_type.71) | copy-start | bytes 25165828
  116.1 2.2 copy-start.2
  119.8 3.4 %copy-start.1 = (bf16[16384,128]{0,1:T(8,128)(2,1)}, bf16[16384,128]{0,1:T(8,128)(2,1)S(1)}, u32[]{:S(2)}) copy-start(bf16[16384,128]{0,1:T(8,128)(2,1)S(1)} %add_convert_fusion) | copy-start | bytes 12582916
  203.2 13.5 %all-to-all-start.2 = ((bf16[16,64,128]{2,1,0:T(8,128)(2,1)}), bf16[16,64,128]{2,1,0:T(8,128)(2,1)S(1)}, u32[]{:S(2)}, u32[]{:S(2)}) async-start(bf16[16,64,128]{2,1,0:T(8,128)(2,1)} %subtract_convert_fusion.1), calls=%async_computation.2 | async-start | bytes 524288 | tf_op jit(solution)/shard_map/all_to_all | solution.py:109
Sparse Core Ops, SparseCore 0:
  10.2 55.6 all-gather.1
where the time goes:
time: 228 us; the launch traced here: 225 us
  other arithmetic  83.3 us (37%)
  local copies, waits for them, and re-layouts  74.5 us (33%)
  waiting for transfers between devices  19.4 us (9%)
  starting transfers between devices  17.4 us (8%)
  matrix products  15.9 us (7%)
  between operations  14.9 us (7%)
    concatenate x6, local copies, waits for them, and re-layouts, along_axis(): jnp.concatenate([leading[..., :midway] - second[..., midway:], leading[.....  23.2 us
    another operation x8, other arithmetic  21.6 us
    sub x1, other arithmetic, complex_product(): left_real * right_real - left_imaginary * right_imaginary  18.7 us
    unnamed x9, local copies, waits for them, and re-layouts  17.5 us
    concatenate x2, local copies, waits for them, and re-layouts, complex_product(): jnp.concatenate([left_real * right_real - left_imaginary * right_imaginar...  12.2 us
    concatenate x2, other arithmetic, complex_product(): jnp.concatenate([left_real * right_real - left_imaginary * right_imaginar...  11.4 us
    all_to_all x1, waiting for transfers between devices, body(): lax.all_to_all(send_rows.reshape(peer_count, capacity, columns), 'facet',...  10.2 us
    scatter-add x1, other arithmetic, body(): jax.ops.segment_sum(slot_wide, cell_ids, num_segments=CELLS + 1)[:CELLS]  9.78 us
  transfers between devices with their start and end apart: 4, of which 3 were waited for; matrix products, arithmetic and copies ran while one was open for 15% of the time, Pallas kernels for 0%

commit v1 on v0

v1 whole, which is shorter than its diff:
```python
import functools
import math

import jax
import jax.numpy as jnp
from jax import lax
from jax.experimental import pallas as pl
from jax.experimental.pallas import tpu as pltpu
from jax.sharding import PartitionSpec as P

LOOP_GAIN = 0.1


def dft_table(length, orient):
    ordinal = jnp.arange(length, dtype=jnp.int32)
    phases = ordinal[:, None] * ordinal[None, :] % length
    angles = phases.astype(jnp.float32) * (2.0 * math.pi / length)
    return jnp.concatenate([jnp.cos(angles), orient * jnp.sin(angles)], 1).astype(jnp.bfloat16)


def turned(values):
    half = values.shape[-1] // 2
    lane = lax.broadcasted_iota(jnp.int32, values.shape, 1)
    rolled = pltpu.roll(values, half, 1)
    return jnp.where(lane < half, -rolled, rolled)


def stage(table, first, second):
    top = jnp.concatenate([first, second], 1).astype(jnp.bfloat16)
    low = jnp.concatenate([turned(first), turned(second)], 1).astype(jnp.bfloat16)
    return jnp.dot(table, jnp.concatenate([top, low], 0), preferred_element_type=jnp.float32)


def cycle_kernel(gu, gv, grid_at, panel_at, scale, rows, panel, model, minus, plus,
                 model_next, answer, wide, cross, picked):
    cells = gu * gv
    slots, columns = rows.shape
    half = columns // 2

    chunk = 512

    @pl.loop(0, cells // chunk)
    def _(i):
        at = pl.ds(pl.multiple_of(i * chunk, chunk), chunk)
        wide[at, :] = jnp.zeros((chunk, columns), jnp.float32)
        cross[at, :] = panel[at, :].astype(jnp.float32)

    wide[pl.ds(cells, 8), :] = jnp.zeros((8, columns), jnp.float32)

    @pl.loop(0, slots // 16)
    def _(i):
        base = pl.multiple_of(i * 16, 16)
        for k in range(16):
            picked[pl.ds(base + k, 1), :] = cross[pl.ds(panel_at[base + k], 1), :]

    lane = lax.broadcasted_iota(jnp.int32, (slots, columns), 1)
    kernel_rows = picked[...]
    swapped = pltpu.roll(kernel_rows, half, 1)
    real = jnp.where(lane < half, kernel_rows, swapped)
    imag = jnp.where(lane < half, swapped, kernel_rows)
    values = rows[...].astype(jnp.float32)
    cross[pl.ds(0, slots), :] = values * real + turned(values) * imag

    @pl.loop(0, slots // 16)
    def _(i):
        base = pl.multiple_of(i * 16, 16)
        for k in range(16):
            at = pl.ds(grid_at[base + k], 1)
            wide[at, :] += cross[pl.ds(base + k, 1), :]

    @pl.loop(0, gv // 2)
    def _(i):
        base = pl.multiple_of(i * (2 * gu), 2 * gu)
        out = stage(minus[...], wide[pl.ds(base, gu), :], wide[pl.ds(base + gu, gu), :])
        cross[pl.ds(2 * i, gu, stride=gv), :] = out[:, :columns]
        cross[pl.ds(2 * i + 1, gu, stride=gv), :] = out[:, columns:]

    gain = scale[0]

    @pl.loop(0, gu // 2)
    def _(i):
        base = pl.multiple_of(i * (2 * gv), 2 * gv)
        low, high = pl.ds(base, gv), pl.ds(base + gv, gv)
        out = stage(minus[...], cross[low, :], cross[high, :])
        first = (model[low, :].astype(jnp.float32) + gain * out[:, :columns]).astype(jnp.bfloat16)
        second = (model[high, :].astype(jnp.float32) + gain * out[:, columns:]).astype(jnp.bfloat16)
        model_next[low, :] = first
        model_next[high, :] = second
        out = stage(plus[...], first.astype(jnp.float32), second.astype(jnp.float32))
        wide[pl.ds(2 * i, gv, stride=gu), :] = out[:, :columns]
        wide[pl.ds(2 * i + 1, gv, stride=gu), :] = out[:, columns:]

    @pl.loop(0, gv // 2)
    def _(i):
        base = pl.multiple_of(i * (2 * gu), 2 * gu)
        out = stage(plus[...], wide[pl.ds(base, gu), :], wide[pl.ds(base + gu, gu), :])
        cross[pl.ds(base, gu), :] = out[:, :columns]
        cross[pl.ds(base + gu, gu), :] = out[:, columns:]

    cross[pl.ds(cells, 8), :] = jnp.zeros((8, columns), jnp.float32)

    @pl.loop(0, slots // 16)
    def _(i):
        base = pl.multiple_of(i * 16, 16)
        for k in range(16):
            wide[pl.ds(base + k, 1), :] = cross[pl.ds(grid_at[base + k], 1), :]

    kernel_rows = picked[...]
    swapped = pltpu.roll(kernel_rows, half, 1)
    real = jnp.where(lane < half, kernel_rows, swapped)
    imag = jnp.where(lane < half, swapped, kernel_rows)
    found = wide[pl.ds(0, slots), :] * (1.0 / math.sqrt(cells))
    predicted = found * real - turned(found) * imag
    answer[...] = (rows[...].astype(jnp.float32) - predicted).astype(jnp.bfloat16)


def run_cycle(gu, gv, grid_at, panel_at, scale, rows, panel, model):
    cells = gu * gv
    slots, columns = rows.shape
    smem = pl.BlockSpec(memory_space=pltpu.SMEM)
    vmem = pl.BlockSpec(memory_space=pltpu.VMEM)
    return pl.pallas_call(
        functools.partial(cycle_kernel, gu, gv),
        out_shape=(
            jax.ShapeDtypeStruct((cells, columns), jnp.bfloat16),
            jax.ShapeDtypeStruct((slots, columns), jnp.bfloat16),
        ),
        in_specs=[smem] * 3 + [vmem] * 5,
        out_specs=(vmem, vmem),
        scratch_shapes=[
            pltpu.VMEM((cells + 8, columns), jnp.float32),
            pltpu.VMEM((cells + 8, columns), jnp.float32),
            pltpu.VMEM((slots, columns), jnp.float32),
        ],
        compiler_params=pltpu.CompilerParams(vmem_limit_bytes=50 * 1024 * 1024),
    )(grid_at, panel_at, scale, rows, panel, model, dft_table(gu, -1), dft_table(gu, 1))


def body(visibility, facet_of, cell_of, taper, model):
    peers = lax.axis_size("facet")
    local_rows, columns = visibility.shape
    capacity = 2 * local_rows // peers
    slots = peers * capacity
    cells = model.shape[0]
    gu = gv = math.isqrt(cells)

    panel = lax.all_gather(taper, "facet", axis=0, tiled=True)

    target = facet_of[:, 0]
    order = jnp.arange(local_rows, dtype=jnp.int32)
    earlier = (order[:, None] > order[None, :]) & (target[:, None] == target[None, :])
    position = target * capacity + jnp.sum(earlier.astype(jnp.int32), axis=1)
    placed = jnp.arange(slots, dtype=jnp.int32)[:, None] == position[None, :]
    send_rows = jnp.dot(
        placed.astype(jnp.bfloat16), visibility, preferred_element_type=jnp.float32
    ).astype(jnp.bfloat16)
    send_cells = jnp.min(jnp.where(placed, cell_of[None, :], cells), axis=1)

    cell_ids = lax.all_to_all(
        send_cells.reshape(peers, capacity), "facet", split_axis=0, concat_axis=0, tiled=True
    ).reshape(slots)
    rows = lax.all_to_all(
        send_rows.reshape(peers, capacity, columns), "facet", split_axis=0, concat_axis=0, tiled=True
    ).reshape(slots, columns)

    used = cell_ids < cells
    scale = LOOP_GAIN / jnp.sqrt(jnp.sum(used.astype(jnp.float32)))
    grid_at = jnp.where(used, cell_ids % gv * gu + cell_ids // gv, cells)
    panel_at = jnp.minimum(cell_ids, cells - 1)
    model_next, answer = run_cycle(gu, gv, grid_at, panel_at, scale.reshape(1), rows, panel, model)

    returned = lax.all_to_all(
        answer.reshape(peers, capacity, columns), "facet", split_axis=0, concat_axis=0, tiled=True
    ).reshape(slots, columns)
    residual = lax.dot_general(
        placed.astype(jnp.bfloat16), returned, (((0,), (0,)), ((), ())),
        preferred_element_type=jnp.float32,
    ).astype(jnp.bfloat16)
    return (model_next, residual)


def solution(mesh):
    both = ("groups", "facet")
    return jax.shard_map(
        body,
        mesh=mesh,
        in_specs=(P(both, None), P(both, None), P(both), P(both, None), P(both, None)),
        out_specs=(P(both, None), P(both, None)),
        check_vma=False,
    )
```

time: 228 us -> 174 us (0.76)
  Pallas kernels: 0 us -> 84.4 us
  other arithmetic: 83.3 us -> 4.57 us
  local copies, waits for them, and re-layouts: 74.5 us -> 1.27 us
  waiting for transfers between devices: 19.4 us -> 40.4 us
  blocking collectives: 0 us -> 13.4 us
  matrix products: 15.9 us -> 2.6 us
  starting transfers between devices: 17.4 us -> 11.5 us
    pallas_call x0 -> x1, Pallas kernels: none -> 84.4 us  [run_cycle(): pl.pallas_call(functools.partial(cycle_kernel, gu, gv), out_shape=(jax.Sh...]
    concatenate x8 -> x0, local copies, waits for them, and re-layouts: 35.3 us -> none  [the longest x6 23.2 us: along_axis(): jnp.concatenate([leading[..., :midway] - second[..., midway:], leading[.....]
    all_gather x1, waiting for transfers between devices: 5.42 us -> 27.7 us  [body(): panel = lax.all_gather(taper, 'facet', axis=0, tiled=True)]
    another operation x8 -> x2, other arithmetic: 21.6 us -> 0.54 us
    sub x1 -> x0, other arithmetic: 18.7 us -> none  [complex_product(): left_real * right_real - left_imaginary * right_imaginary]
    unnamed x9 -> x2, local copies, waits for them, and re-layouts: 17.5 us -> 0.01 us
    concatenate x4 -> x1, other arithmetic: 16 us -> 0.02 us  [dft_table(): jnp.concatenate([jnp.cos(angles), orient * jnp.sin(angles)], 1)]
    all_to_all x0 -> x1, blocking collectives: none -> 13.4 us  [body(): lax.all_to_all(answer.reshape(peers, capacity, columns), 'facet', split_a...]
  transfers between devices with their start and end apart: 4 -> 3, of which waited for: 3 -> 3; matrix products, arithmetic and copies ran while one was open for 15% -> 4% of each run, Pallas kernels for 0% -> 0%
where the time goes in v1:
time: 174 us; the launch traced here: 173 us
  Pallas kernels  84.4 us (49%)
  waiting for transfers between devices  40.4 us (23%)
  between operations  14.8 us (9%)
  blocking collectives  13.4 us (8%)
  starting transfers between devices  11.5 us (7%)
  other arithmetic  4.57 us (3%)
  matrix products  2.6 us (1%)
    pallas_call x1, Pallas kernels, run_cycle(): pl.pallas_call(functools.partial(cycle_kernel, gu, gv), out_shape=(jax.Sh...  84.4 us
    all_gather x1, waiting for transfers between devices, body(): panel = lax.all_gather(taper, 'facet', axis=0, tiled=True)  27.7 us
    all_to_all x1, blocking collectives, body(): lax.all_to_all(answer.reshape(peers, capacity, columns), 'facet', split_a...  13.4 us
    all_to_all x1, waiting for transfers between devices, body(): lax.all_to_all(send_rows.reshape(peers, capacity, columns), 'facet', spli...  7.69 us
    all_to_all x1, starting transfers between devices, body(): lax.all_to_all(send_cells.reshape(peers, capacity), 'facet', split_axis=0...  7.35 us
    all_to_all x1, waiting for transfers between devices, body(): lax.all_to_all(send_cells.reshape(peers, capacity), 'facet', split_axis=0...  4.26 us
    all_to_all x1, starting transfers between devices, body(): lax.all_to_all(send_rows.reshape(peers, capacity, columns), 'facet', spli...  4.12 us
  transfers between devices with their start and end apart: 3, of which 3 were waited for; matrix products, arithmetic and copies ran while one was open for 4% of the time, Pallas kernels for 0%

profile of v1, /device:TPU:1, one launch (start us, length us, event | category | flops | bytes accessed | tf_op | source)
XLA Modules:
  0.0 172.9 jit_solution(882922610477144325)
XLA Ops:
  7.2 0.0 copy-start
  7.2 0.0 all-gather.2.cloned.1.call-start
  7.2 0.7 all-gather.2.cloned.1.call-update
  7.9 1.0 convert_reduce_fusion
  8.9 0.7 multiply_add_fusion
  9.6 1.0 select_reduce_fusion
  10.6 0.7 all_to_all.12
  11.3 7.3 %all-to-all-start = ((s32[16,1,64]{2,1,0:T(1,128)}), s32[16,1,64]{2,1,0:T(1,128)S(1)}, u32[]{:S(2)}, u32[]{:S(2)}) async-start(s32[16,1,64]{2,1,0:T(1,128)} %all_to_all.12), calls=%async_computation | async-start | bytes 16384 | tf_op jit(solution)/shard_map/all_to_all | solution.py:159
  18.7 0.0 copy-done
  18.7 1.2 fusion.2
  19.8 0.3 multiply_convert_fusion
  20.1 4.3 %all-to-all-done = s32[16,1,64]{2,1,0:T(1,128)S(1)} async-done(((s32[16,1,64]{2,1,0:T(1,128)}), s32[16,1,64]{2,1,0:T(1,128)S(1)}, u32[]{:S(2)}, u32[]{:S(2)}) %all-to-all-start) | async-done | bytes 4128 | tf_op jit(solution)/shard_map/all_to_all | solution.py:159
  24.4 4.1 %all-to-all-start.1 = ((bf16[16,64,128]{2,1,0:T(8,128)(2,1)}), bf16[16,64,128]{2,1,0:T(8,128)(2,1)S(1)}, u32[]{:S(2)}, u32[]{:S(2)}) async-start(bf16[16,64,128]{2,1,0:T(8,128)(2,1)} %bitcast.3), calls=%async_computation.1 | async-start | bytes 524288 | tf_op jit(solution)/shard_map/all_to_all | solution.py:162
  28.5 0.3 fusion.14
  28.8 0.6 convert_reduce_fusion.1
  30.1 0.5 broadcast.54
  30.6 0.7 reduce.5
  31.3 0.1 reshape.40
  31.4 7.7 %all-to-all-done.1 = bf16[16,64,128]{2,1,0:T(8,128)(2,1)S(1)} async-done(((bf16[16,64,128]{2,1,0:T(8,128)(2,1)}), bf16[16,64,128]{2,1,0:T(8,128)(2,1)S(1)}, u32[]{:S(2)}, u32[]{:S(2)}) %all-to-all-start.1) | async-done | bytes 262176 | tf_op jit(solution)/shard_map/all_to_all | solution.py:162
  39.1 27.7 %all-gather.2.cloned.1.call-done.panel = bf16[16384,128]{1,0:T(8,128)(2,1)} async-done(((bf16[1024,128]{1,0:T(8,128)(2,1)}), bf16[16384,128]{1,0:T(8,128)(2,1)}) %all-gather.2.cloned.1.call-update) | async-done | bytes 4194320 | tf_op jit(solution)/shard_map/all_gather | solution.py:147
  66.8 84.4 %shard_map.68 = (bf16[16384,128]{1,0:T(8,128)(2,1)}, bf16[1024,128]{1,0:T(8,128)(2,1)S(1)}) custom-call(s32[1024]{0:T(1024)S(1)} %get-tuple-element.9.grid_at, s32[1024]{0:T(1024)S(1)} %get-tuple-element.8.panel_at, f32[1]{0:T(128)} %bitcast.2.scale, bf16[1024,128]{1,0:T(8,128)(2,1)S(1)} %bitcast.9, bf16[16384,128]{1,0:T(8,128)(2,1)} %all-gather.2.cloned.1.call-done.panel, ...), custom_call_target="tpu_custom_call" | custom-call | tf_op jit(solution)/shard_map/pallas_call | solution.py:122
  151.2 13.4 %all_to_all.19 = bf16[16,64,128]{2,1,0:T(8,128)(2,1)S(1)} all-to-all(bf16[16,64,128]{2,1,0:T(8,128)(2,1)S(1)} %bitcast.10), channel_id=1, replica_groups=mesh['groups'=2,'facet'=16] {'facet'}, dimensions={0} | all-to-all | bytes 524288 | tf_op jit(solution)/shard_map/all_to_all | solution.py:172
  164.7 1.4 fusion.3
  (2 shorter events, 0.0 us)
Async XLA Ops:
  7.2 11.5 %copy-start = (bf16[512,128]{1,0:T(8,128)(2,1)S(1)}, bf16[512,128]{1,0:T(8,128)(2,1)}, u32[]{:S(2)}) copy-start(bf16[512,128]{1,0:T(8,128)(2,1)} %param.5) | copy-start | bytes 393220
  7.2 59.6 %all-gather.2.cloned.1.call-start = ((), (), s32[]{:S(2)}) async-start(), calls=%async_computation.3 | async-start | bytes 4456448 | tf_op jit(solution)/shard_map/all_gather | solution.py:147
  11.3 13.1 %all-to-all-start = ((s32[16,1,64]{2,1,0:T(1,128)}), s32[16,1,64]{2,1,0:T(1,128)S(1)}, u32[]{:S(2)}, u32[]{:S(2)}) async-start(s32[16,1,64]{2,1,0:T(1,128)} %all_to_all.12), calls=%async_computation | async-start | bytes 16384 | tf_op jit(solution)/shard_map/all_to_all | solution.py:159
  24.4 14.7 %all-to-all-start.1 = ((bf16[16,64,128]{2,1,0:T(8,128)(2,1)}), bf16[16,64,128]{2,1,0:T(8,128)(2,1)S(1)}, u32[]{:S(2)}, u32[]{:S(2)}) async-start(bf16[16,64,128]{2,1,0:T(8,128)(2,1)} %bitcast.3), calls=%async_computation.1 | async-start | bytes 524288 | tf_op jit(solution)/shard_map/all_to_all | solution.py:162
Sparse Core Ops, SparseCore 0:
  10.2 56.5 all-gather.1

commit v2 on v1

--- a/solution.py
+++ b/solution.py
@@ -9,6 +9,8 @@
 from jax.sharding import PartitionSpec as P
 
 LOOP_GAIN = 0.1
+GROUP = 8
+UNROLL = 2
 
 
 def dft_table(length, orient):
@@ -25,10 +27,12 @@
     return jnp.where(lane < half, -rolled, rolled)
 
 
-def stage(table, first, second):
-    top = jnp.concatenate([first, second], 1).astype(jnp.bfloat16)
-    low = jnp.concatenate([turned(first), turned(second)], 1).astype(jnp.bfloat16)
-    return jnp.dot(table, jnp.concatenate([top, low], 0), preferred_element_type=jnp.float32)
+def stage(table, slabs):
+    columns = slabs[0].shape[1]
+    top = jnp.concatenate(slabs, 1).astype(jnp.bfloat16)
+    low = jnp.concatenate([turned(slab) for slab in slabs], 1).astype(jnp.bfloat16)
+    out = jnp.dot(table, jnp.concatenate([top, low], 0), preferred_element_type=jnp.float32)
+    return [out[:, k * columns : (k + 1) * columns] for k in range(len(slabs))]
 
 
 def cycle_kernel(gu, gv, grid_at, panel_at, scale, rows, panel, model, minus, plus,
@@ -68,34 +72,35 @@
             at = pl.ds(grid_at[base + k], 1)
             wide[at, :] += cross[pl.ds(base + k, 1), :]
 
-    @pl.loop(0, gv // 2)
+    @pl.loop(0, gv // GROUP, unroll=UNROLL)
     def _(i):
-        base = pl.multiple_of(i * (2 * gu), 2 * gu)
-        out = stage(minus[...], wide[pl.ds(base, gu), :], wide[pl.ds(base + gu, gu), :])
-        cross[pl.ds(2 * i, gu, stride=gv), :] = out[:, :columns]
-        cross[pl.ds(2 * i + 1, gu, stride=gv), :] = out[:, columns:]
+        base = pl.multiple_of(i * (GROUP * gu), GROUP * gu)
+        out = stage(minus[...], [wide[pl.ds(base + k * gu, gu), :] for k in range(GROUP)])
+        for k in range(GROUP):
+            cross[pl.ds(GROUP * i + k, gu, stride=gv), :] = out[k]
 
     gain = scale[0]
 
-    @pl.loop(0, gu // 2)
+    @pl.loop(0, gu // GROUP, unroll=UNROLL)
     def _(i):
-        base = pl.multiple_of(i * (2 * gv), 2 * gv)
-        low, high = pl.ds(base, gv), pl.ds(base + gv, gv)
-        out = stage(minus[...], cross[low, :], cross[high, :])
-        first = (model[low, :].astype(jnp.float32) + gain * out[:, :columns]).astype(jnp.bfloat16)
-        second = (model[high, :].astype(jnp.float32) + gain * out[:, columns:]).astype(jnp.bfloat16)
-        model_next[low, :] = first
-        model_next[high, :] = second
-        out = stage(plus[...], first.astype(jnp.float32), second.astype(jnp.float32))
-        wide[pl.ds(2 * i, gv, stride=gu), :] = out[:, :columns]
-        wide[pl.ds(2 * i + 1, gv, stride=gu), :] = out[:, columns:]
+        base = pl.multiple_of(i * (GROUP * gv), GROUP * gv)
+        at = [pl.ds(base + k * gv, gv) for k in range(GROUP)]
+        out = stage(minus[...], [cross[here, :] for here in at])
+        updated = []
+        for k in range(GROUP):
+            value = (model[at[k], :].astype(jnp.float32) + gain * out[k]).astype(jnp.bfloat16)
+            model_next[at[k], :] = value
+            updated.append(value.astype(jnp.float32))
+        out = stage(plus[...], updated)
+        for k in range(GROUP):
+            wide[pl.ds(GROUP * i + k, gv, stride=gu), :] = out[k]
 
-    @pl.loop(0, gv // 2)
+    @pl.loop(0, gv // GROUP, unroll=UNROLL)
     def _(i):
-        base = pl.multiple_of(i * (2 * gu), 2 * gu)
-        out = stage(plus[...], wide[pl.ds(base, gu), :], wide[pl.ds(base + gu, gu), :])
-        cross[pl.ds(base, gu), :] = out[:, :columns]
-        cross[pl.ds(base + gu, gu), :] = out[:, columns:]
+        base = pl.multiple_of(i * (GROUP * gu), GROUP * gu)
+        out = stage(plus[...], [wide[pl.ds(base + k * gu, gu), :] for k in range(GROUP)])
+        for k in range(GROUP):
+            cross[pl.ds(base + k * gu, gu), :] = out[k]
 
     cross[pl.ds(cells, 8), :] = jnp.zeros((8, columns), jnp.float32)
 

time: 174 us -> 128 us (0.74)
  Pallas kernels: 84.4 us -> 38.7 us
    pallas_call x1, Pallas kernels: 84.4 us -> 38.7 us  [run_cycle(): pl.pallas_call(functools.partial(cycle_kernel, gu, gv), out_shape=(jax.Sh...]
  transfers between devices with their start and end apart: 3 -> 3, of which waited for: 3 -> 3; matrix products, arithmetic and copies ran while one was open for 4% -> 5% of each run, Pallas kernels for 0% -> 0%
where the time goes in v2:
time: 128 us; the launch traced here: 127 us
  waiting for transfers between devices  40.4 us (32%)
  Pallas kernels  38.7 us (30%)
  between operations  14.8 us (12%)
  blocking collectives  13 us (10%)
  starting transfers between devices  11.5 us (9%)
  other arithmetic  4.57 us (4%)
  matrix products  2.6 us (2%)
    pallas_call x1, Pallas kernels, run_cycle(): pl.pallas_call(functools.partial(cycle_kernel, gu, gv), out_shape=(jax.Sh...  38.7 us
    all_gather x1, waiting for transfers between devices, body(): panel = lax.all_gather(taper, 'facet', axis=0, tiled=True)  27.7 us
    all_to_all x1, blocking collectives, body(): lax.all_to_all(answer.reshape(peers, capacity, columns), 'facet', split_a...  13 us
    all_to_all x1, waiting for transfers between devices, body(): lax.all_to_all(send_rows.reshape(peers, capacity, columns), 'facet', spli...  7.69 us
    all_to_all x1, starting transfers between devices, body(): lax.all_to_all(send_cells.reshape(peers, capacity), 'facet', split_axis=0...  7.35 us
    all_to_all x1, waiting for transfers between devices, body(): lax.all_to_all(send_cells.reshape(peers, capacity), 'facet', split_axis=0...  4.26 us
    all_to_all x1, starting transfers between devices, body(): lax.all_to_all(send_rows.reshape(peers, capacity, columns), 'facet', spli...  4.12 us
  transfers between devices with their start and end apart: 3, of which 3 were waited for; matrix products, arithmetic and copies ran while one was open for 5% of the time, Pallas kernels for 0%

profile of v2, /device:TPU:1, one launch (start us, length us, event | category | flops | bytes accessed | tf_op | source)
XLA Modules:
  0.0 126.8 jit_solution(14407294486261085127)
XLA Ops:
  7.2 0.0 copy-start
  7.2 0.0 all-gather.2.cloned.1.call-start
  7.2 0.7 all-gather.2.cloned.1.call-update
  7.9 1.0 convert_reduce_fusion
  8.9 0.7 multiply_add_fusion
  9.6 1.0 select_reduce_fusion
  10.6 0.7 all_to_all.12
  11.3 7.3 %all-to-all-start = ((s32[16,1,64]{2,1,0:T(1,128)}), s32[16,1,64]{2,1,0:T(1,128)S(1)}, u32[]{:S(2)}, u32[]{:S(2)}) async-start(s32[16,1,64]{2,1,0:T(1,128)} %all_to_all.12), calls=%async_computation | async-start | bytes 16384 | tf_op jit(solution)/shard_map/all_to_all | solution.py:164
  18.7 0.0 copy-done
  18.7 1.2 fusion.2
  19.8 0.3 multiply_convert_fusion
  20.1 4.3 %all-to-all-done = s32[16,1,64]{2,1,0:T(1,128)S(1)} async-done(((s32[16,1,64]{2,1,0:T(1,128)}), s32[16,1,64]{2,1,0:T(1,128)S(1)}, u32[]{:S(2)}, u32[]{:S(2)}) %all-to-all-start) | async-done | bytes 4128 | tf_op jit(solution)/shard_map/all_to_all | solution.py:164
  24.4 4.1 %all-to-all-start.1 = ((bf16[16,64,128]{2,1,0:T(8,128)(2,1)}), bf16[16,64,128]{2,1,0:T(8,128)(2,1)S(1)}, u32[]{:S(2)}, u32[]{:S(2)}) async-start(bf16[16,64,128]{2,1,0:T(8,128)(2,1)} %bitcast.3), calls=%async_computation.1 | async-start | bytes 524288 | tf_op jit(solution)/shard_map/all_to_all | solution.py:167
  28.5 0.3 fusion.14
  28.8 0.6 convert_reduce_fusion.1
  30.1 0.5 broadcast.54
  30.6 0.7 reduce.5
  31.3 0.1 reshape.40
  31.4 7.7 %all-to-all-done.1 = bf16[16,64,128]{2,1,0:T(8,128)(2,1)S(1)} async-done(((bf16[16,64,128]{2,1,0:T(8,128)(2,1)}), bf16[16,64,128]{2,1,0:T(8,128)(2,1)S(1)}, u32[]{:S(2)}, u32[]{:S(2)}) %all-to-all-start.1) | async-done | bytes 262176 | tf_op jit(solution)/shard_map/all_to_all | solution.py:167
  39.1 27.7 %all-gather.2.cloned.1.call-done.panel = bf16[16384,128]{1,0:T(8,128)(2,1)} async-done(((bf16[1024,128]{1,0:T(8,128)(2,1)}), bf16[16384,128]{1,0:T(8,128)(2,1)}) %all-gather.2.cloned.1.call-update) | async-done | bytes 4194320 | tf_op jit(solution)/shard_map/all_gather | solution.py:152
  66.8 38.7 %shard_map.68 = (bf16[16384,128]{1,0:T(8,128)(2,1)}, bf16[1024,128]{1,0:T(8,128)(2,1)S(1)}) custom-call(s32[1024]{0:T(1024)S(1)} %get-tuple-element.9.grid_at, s32[1024]{0:T(1024)S(1)} %get-tuple-element.8.panel_at, f32[1]{0:T(128)} %bitcast.2.scale, bf16[1024,128]{1,0:T(8,128)(2,1)S(1)} %bitcast.9, bf16[16384,128]{1,0:T(8,128)(2,1)} %all-gather.2.cloned.1.call-done.panel, ...), custom_call_target="tpu_custom_call" | custom-call | tf_op jit(solution)/shard_map/pallas_call | solution.py:127
  105.5 13.0 %all_to_all.19 = bf16[16,64,128]{2,1,0:T(8,128)(2,1)S(1)} all-to-all(bf16[16,64,128]{2,1,0:T(8,128)(2,1)S(1)} %bitcast.10), channel_id=1, replica_groups=mesh['groups'=2,'facet'=16] {'facet'}, dimensions={0} | all-to-all | bytes 524288 | tf_op jit(solution)/shard_map/all_to_all | solution.py:177
  118.5 1.4 %fusion.3 = bf16[512,128]{1,0:T(8,128)(2,1)} fusion(bf16[1024,128]{1,0:T(8,128)(2,1)S(1)} %bitcast.11, s32[512]{0:T(512)S(1)} %multiply_add_fusion), kind=kOutput, calls=%fused_computation.5 | convolution fusion | flops 134807552 | bytes 395264 | tf_op jit(solution)/shard_map/dot_general | solution.py:180
  (2 shorter events, 0.0 us)
Async XLA Ops:
  7.2 11.5 %copy-start = (bf16[512,128]{1,0:T(8,128)(2,1)S(1)}, bf16[512,128]{1,0:T(8,128)(2,1)}, u32[]{:S(2)}) copy-start(bf16[512,128]{1,0:T(8,128)(2,1)} %param.5) | copy-start | bytes 393220
  7.2 59.6 %all-gather.2.cloned.1.call-start = ((), (), s32[]{:S(2)}) async-start(), calls=%async_computation.3 | async-start | bytes 4456448 | tf_op jit(solution)/shard_map/all_gather | solution.py:152
  11.3 13.1 %all-to-all-start = ((s32[16,1,64]{2,1,0:T(1,128)}), s32[16,1,64]{2,1,0:T(1,128)S(1)}, u32[]{:S(2)}, u32[]{:S(2)}) async-start(s32[16,1,64]{2,1,0:T(1,128)} %all_to_all.12), calls=%async_computation | async-start | bytes 16384 | tf_op jit(solution)/shard_map/all_to_all | solution.py:164
  24.4 14.7 %all-to-all-start.1 = ((bf16[16,64,128]{2,1,0:T(8,128)(2,1)}), bf16[16,64,128]{2,1,0:T(8,128)(2,1)S(1)}, u32[]{:S(2)}, u32[]{:S(2)}) async-start(bf16[16,64,128]{2,1,0:T(8,128)(2,1)} %bitcast.3), calls=%async_computation.1 | async-start | bytes 524288 | tf_op jit(solution)/shard_map/all_to_all | solution.py:167
Sparse Core Ops, SparseCore 0:
  10.2 56.5 all-gather.1

commit v3 on v2

--- a/solution.py
+++ b/solution.py
@@ -9,6 +9,7 @@
 from jax.sharding import PartitionSpec as P
 
 LOOP_GAIN = 0.1
+MESH = pl.DeviceIdType.MESH
 GROUP = 8
 UNROLL = 2
 
@@ -141,6 +142,152 @@
     )(grid_at, panel_at, scale, rows, panel, model, dft_table(gu, -1), dft_table(gu, 1))
 
 
+def greet(peers):
+    me = lax.axis_index("facet")
+    barrier = pltpu.get_barrier_semaphore()
+    for step in range(1, peers):
+        pl.semaphore_signal(
+            barrier, inc=1, device_id={"facet": lax.rem(me + step, peers)}, device_id_type=MESH
+        )
+    pl.semaphore_wait(barrier, peers - 1)
+
+
+def sent(source, target, send_sem, recv_sem, peer):
+    copy = pltpu.make_async_remote_copy(
+        src_ref=source, dst_ref=target, send_sem=send_sem, recv_sem=recv_sem,
+        device_id={"facet": peer}, device_id_type=MESH,
+    )
+    copy.start()
+    return copy
+
+
+def swap_blocks(peers, source, target, send_sems, recv_sems):
+    me = lax.axis_index("facet")
+    copies = []
+    for step in range(1, peers):
+        peer = lax.rem(me + step, peers)
+        copies.append(
+            sent(source.at[peer], target.at[me], send_sems.at[step], recv_sems.at[step], peer)
+        )
+    return copies
+
+
+def chip_at(place, chips):
+    if chips != 8:
+        return place
+    back = place // 4
+    return (1 - back) * (2 * place) + back * (15 - 2 * place)
+
+
+def place_of(chip, chips):
+    if chips != 8:
+        return chip
+    return chip // 2 + (chip % 2) * (7 - 2 * (chip // 2))
+
+
+def spread_kernel(peers, rows, ids, taper, rows_out, ids_out, panel, own_sems, row_send, row_recv,
+                  id_send, id_recv, ring_send, ring_recv, pass_send, pass_recv):
+    me = lax.axis_index("facet")
+    chips = peers // 2
+    core, place = lax.rem(me, 2), place_of(me // 2, chips)
+    sibling = me + 1 - 2 * core
+    depth = taper.shape[0]
+    half = depth // 2
+
+    def owner(distance):
+        return chip_at(lax.rem(place + distance + chips, chips), chips) * 2 + core
+
+    right, left = owner(1), owner(-1)
+    greet(peers)
+
+    own = [
+        pltpu.make_async_copy(rows.at[me], rows_out.at[me], own_sems.at[0]),
+        pltpu.make_async_copy(ids.at[me], ids_out.at[me], own_sems.at[1]),
+        pltpu.make_async_copy(taper, panel.at[me], own_sems.at[2]),
+    ]
+
+    def ring(way, step, peer):
+        if step == 0:
+            source, target = taper, panel.at[me]
+        else:
+            block = owner(-step if way == 0 else step)
+            source = target = panel.at[block]
+            if step == chips // 2 - 1:
+                part = pl.ds(way * half, half)
+                source = target = panel.at[block, part]
+        return sent(source, target, ring_send.at[way, step], ring_recv.at[way, step], peer)
+
+    started = []
+    going = [ring(0, 0, right), ring(1, 0, left)]
+    moves = swap_blocks(peers, ids, ids_out, id_send, id_recv)
+    moves += swap_blocks(peers, rows, rows_out, row_send, row_recv)
+    passed = [sent(taper, panel.at[me], pass_send.at[0, 0], pass_recv.at[0, 0], sibling)]
+    for copy in own:
+        copy.start()
+    for step in range(chips // 2):
+        arrived = going
+        started += going
+        going = []
+        for way in range(2):
+            arrived[way].wait_recv()
+            if step + 1 < chips // 2:
+                going.append(ring(way, step + 1, right if way == 0 else left))
+            block = owner(-(step + 1) if way == 0 else step + 1)
+            fresh = panel.at[block]
+            if step == chips // 2 - 1:
+                fresh = panel.at[block, pl.ds(way * half, half)]
+            at = (way, step + 1)
+            passed.append(sent(fresh, fresh, pass_send.at[at], pass_recv.at[at], sibling))
+    for copy in started:
+        copy.wait_send()
+    for copy in moves + passed:
+        copy.wait()
+    for copy in own:
+        copy.wait()
+
+
+def spread(peers, rows, ids, taper):
+    steps = peers // 4
+    hbm = pl.BlockSpec(memory_space=pl.ANY)
+    dma = pltpu.SemaphoreType.DMA
+    return pl.pallas_call(
+        functools.partial(spread_kernel, peers),
+        out_shape=(
+            jax.ShapeDtypeStruct(rows.shape, rows.dtype),
+            jax.ShapeDtypeStruct(ids.shape, ids.dtype),
+            jax.ShapeDtypeStruct((peers,) + taper.shape, taper.dtype),
+        ),
+        in_specs=[hbm] * 3,
+        out_specs=(hbm,) * 3,
+        scratch_shapes=[dma((3,))] + [dma((peers,))] * 4 + [dma((2, steps))] * 2
+        + [dma((2, steps + 1))] * 2,
+        compiler_params=pltpu.CompilerParams(collective_id=0, has_side_effects=True),
+    )(rows, ids, taper)
+
+
+def back_kernel(peers, answer, returned, own_sem, send_sems, recv_sems):
+    me = lax.axis_index("facet")
+    own = pltpu.make_async_copy(answer.at[me], returned.at[me], own_sem)
+    own.start()
+    greet(peers)
+    for copy in swap_blocks(peers, answer, returned, send_sems, recv_sems):
+        copy.wait()
+    own.wait()
+
+
+def send_back(peers, answer):
+    hbm = pl.BlockSpec(memory_space=pl.ANY)
+    dma = pltpu.SemaphoreType.DMA
+    return pl.pallas_call(
+        functools.partial(back_kernel, peers),
+        out_shape=jax.ShapeDtypeStruct(answer.shape, answer.dtype),
+        in_specs=[hbm],
+        out_specs=hbm,
+        scratch_shapes=[dma, dma((peers,)), dma((peers,))],
+        compiler_params=pltpu.CompilerParams(collective_id=1, has_side_effects=True),
+    )(answer)
+
+
 def body(visibility, facet_of, cell_of, taper, model):
     peers = lax.axis_size("facet")
     local_rows, columns = visibility.shape
@@ -148,8 +295,6 @@
     slots = peers * capacity
     cells = model.shape[0]
     gu = gv = math.isqrt(cells)
-
-    panel = lax.all_gather(taper, "facet", axis=0, tiled=True)
 
     target = facet_of[:, 0]
     order = jnp.arange(local_rows, dtype=jnp.int32)
@@ -161,12 +306,11 @@
     ).astype(jnp.bfloat16)
     send_cells = jnp.min(jnp.where(placed, cell_of[None, :], cells), axis=1)
 
-    cell_ids = lax.all_to_all(
-        send_cells.reshape(peers, capacity), "facet", split_axis=0, concat_axis=0, tiled=True
-    ).reshape(slots)
-    rows = lax.all_to_all(
-        send_rows.reshape(peers, capacity, columns), "facet", split_axis=0, concat_axis=0, tiled=True
-    ).reshape(slots, columns)
+    ids = jnp.pad(send_cells.reshape(peers, 1, capacity), ((0, 0), (0, 7), (0, 128 - capacity)))
+    rows, ids, panel = spread(peers, send_rows.reshape(peers, capacity, columns), ids, taper)
+    rows = rows.reshape(slots, columns)
+    panel = panel.reshape(cells, columns)
+    cell_ids = ids[:, 0, :capacity].reshape(slots)
 
     used = cell_ids < cells
     scale = LOOP_GAIN / jnp.sqrt(jnp.sum(used.astype(jnp.float32)))
@@ -174,9 +318,7 @@
     panel_at = jnp.minimum(cell_ids, cells - 1)
     model_next, answer = run_cycle(gu, gv, grid_at, panel_at, scale.reshape(1), rows, panel, model)
 
-    returned = lax.all_to_all(
-        answer.reshape(peers, capacity, columns), "facet", split_axis=0, concat_axis=0, tiled=True
-    ).reshape(slots, columns)
+    returned = send_back(peers, answer.reshape(peers, capacity, columns)).reshape(slots, columns)
     residual = lax.dot_general(
         placed.astype(jnp.bfloat16), returned, (((0,), (0,)), ((), ())),
         preferred_element_type=jnp.float32,

time: 128 us -> 102 us (0.80)
  Pallas kernels: 38.7 us -> 87.7 us
  waiting for transfers between devices: 40.4 us -> 0 us
  between operations: 14.8 us -> 1.38 us
  blocking collectives: 13 us -> 0 us
  starting transfers between devices: 11.5 us -> 0 us
  local copies, waits for them, and re-layouts: 1.27 us -> 3.3 us
    pallas_call x0 -> x2, Pallas kernels: none -> 49.2 us  [the longest x1 40.6 us: spread(): pl.pallas_call(functools.partial(spread_kernel, peers), out_shape=(jax.Sh...]
    all_gather x1 -> x0, waiting for transfers between devices: 27.7 us -> none  [body(): panel = lax.all_gather(taper, 'facet', axis=0, tiled=True)]
    all_to_all x1 -> x0, blocking collectives: 13 us -> none  [body(): lax.all_to_all(answer.reshape(peers, capacity, columns), 'facet', split_a...]
    all_to_all x2 -> x0, waiting for transfers between devices: 11.9 us -> none  [the longest x1 7.69 us: body(): lax.all_to_all(send_rows.reshape(peers, capacity, columns), 'facet', spli...]
    all_to_all x2 -> x0, starting transfers between devices: 11.5 us -> none  [the longest x1 7.35 us: body(): lax.all_to_all(send_cells.reshape(peers, capacity), 'facet', split_axis=0...]
    unnamed x2 -> x6, local copies, waits for them, and re-layouts: 0.01 us -> 1.65 us
  transfers between devices with their start and end apart: 3 -> 0, of which waited for: 3 -> 0; matrix products, arithmetic and copies ran while one was open for 5% -> 0% of each run, Pallas kernels for 0% -> 0%
where the time goes in v3:
time: 102 us; the launch traced here: 101 us
  Pallas kernels  87.7 us (86%)
  other arithmetic  4.77 us (5%)
  matrix products  3.55 us (3%)
  local copies, waits for them, and re-layouts  3.3 us (3%)
  between operations  1.38 us (1%)
    pallas_call x1, Pallas kernels, spread(): pl.pallas_call(functools.partial(spread_kernel, peers), out_shape=(jax.Sh...  40.6 us
    pallas_call x1, Pallas kernels, run_cycle(): pl.pallas_call(functools.partial(cycle_kernel, gu, gv), out_shape=(jax.Sh...  38.4 us
    pallas_call x1, Pallas kernels, send_back(): pl.pallas_call(functools.partial(back_kernel, peers), out_shape=jax.Shape...  8.64 us
    dot_general x1, matrix products, body(): lax.dot_general(placed.astype(jnp.bfloat16), returned, (((0,), (0,)), (()...  2.38 us

profile of v3, /device:TPU:1, one launch (start us, length us, event | category | flops | bytes accessed | tf_op | source)
XLA Modules:
  0.0 100.6 jit_solution(12904150747708117675)
XLA Ops:
  0.6 0.0 copy-start
  0.6 1.0 %convert_reduce_fusion = s32[512]{0:T(512)S(1)} fusion(s32[512]{0:T(512)} %bitcast.14), kind=kLoop, calls=%fused_computation.8 | loop fusion | flops 1310208 | bytes 4096 | tf_op jit(solution)/shard_map/reduce_sum | solution.py:302
  1.7 0.7 multiply_add_fusion
  2.3 1.0 %select_reduce_fusion = s32[1024]{0:T(1024)S(1)} fusion(s32[512]{0:T(512)} %param.7, s32[512]{0:T(512)S(1)} %multiply_add_fusion), kind=kLoop, calls=%fused_computation | loop fusion | flops 1571840 | bytes 8192 | tf_op jit(solution)/shard_map/reduce_min | solution.py:307
  3.4 0.1 reshape.36
  3.5 0.3 fusion.14
  3.7 0.6 pad.4.ids
  4.4 0.3 multiply_convert_fusion
  4.7 0.0 copy-done
  4.7 1.2 %fusion.2 = bf16[1024,128]{1,0:T(8,128)(2,1)} fusion(bf16[512,128]{1,0:T(8,128)(2,1)S(1)} %copy-done, s32[512]{0:T(512)S(1)} %multiply_add_fusion), kind=kOutput, calls=%fused_computation.4 | convolution fusion | flops 134873088 | bytes 395264 | tf_op jit(solution)/shard_map/dot_general | solution.py:304
  5.8 40.6 %shard_map.68 = (bf16[16,64,128]{2,1,0:T(8,128)(2,1)}, s32[16,8,128]{2,1,0:T(8,128)}, bf16[16,1024,128]{2,1,0:T(8,128)(2,1)}) custom-call(bf16[16,64,128]{2,1,0:T(8,128)(2,1)} %bitcast.12, s32[16,8,128]{2,1,0:T(8,128)} %pad.4.ids, bf16[1024,128]{1,0:T(8,128)(2,1)} %taper.1), custom_call_target="tpu_custom_call" | custom-call | tf_op jit(solution)/shard_map/pallas_call | solution.py:253
  46.4 1.5 %fusion.15 = f32[]{:T(128)} fusion(s32[16,8,128]{2,1,0:T(8,128)} %get-tuple-element.7), kind=kLoop, calls=%fused_computation.27 | loop fusion | flops 3071 | bytes 4100 | tf_op jit(solution)/shard_map/reduce_sum | solution.py:316
  48.6 0.9 slice_reduce_fusion
  49.5 0.1 reshape_squeeze.3
  49.6 0.0 copy-start.1
  49.6 0.9 copy-done.1
  50.5 38.4 %shard_map.69 = (bf16[16384,128]{1,0:T(8,128)(2,1)}, bf16[1024,128]{1,0:T(8,128)(2,1)S(1)}) custom-call(s32[1024]{0:T(1024)S(1)} %get-tuple-element.15.grid_at, s32[1024]{0:T(1024)S(1)} %get-tuple-element.14.panel_at, f32[1]{0:T(128)} %bitcast.2.scale, bf16[1024,128]{1,0:T(8,128)(2,1)S(1)} %bitcast.9, bf16[16384,128]{1,0:T(8,128)(2,1)} %bitcast.11, ...), custom_call_target="tpu_custom_call" | custom-call | tf_op jit(solution)/shard_map/pallas_call | solution.py:128
  88.9 0.0 copy-start.2
  88.9 0.7 copy-done.2
  89.6 8.6 %shard_map.70 = bf16[16,64,128]{2,1,0:T(8,128)(2,1)} custom-call(bf16[16,64,128]{2,1,0:T(8,128)(2,1)} %bitcast.10), custom_call_target="tpu_custom_call" | custom-call | tf_op jit(solution)/shard_map/pallas_call | solution.py:281
  98.3 2.4 %fusion.3 = bf16[512,128]{1,0:T(8,128)(2,1)} fusion(bf16[1024,128]{1,0:T(8,128)(2,1)} %bitcast.13, s32[512]{0:T(512)S(1)} %multiply_add_fusion), kind=kOutput, calls=%fused_computation.5 | convolution fusion | flops 134807552 | bytes 395264 | tf_op jit(solution)/shard_map/dot_general | solution.py:322
  (2 shorter events, 0.0 us)
Async XLA Ops:
  0.6 4.0 %copy-start = (bf16[512,128]{1,0:T(8,128)(2,1)S(1)}, bf16[512,128]{1,0:T(8,128)(2,1)}, u32[]{:S(2)}) copy-start(bf16[512,128]{1,0:T(8,128)(2,1)} %param.5) | copy-start | bytes 393220
  49.6 1.0 copy-start.1
  88.9 0.7 copy-start.2

commit v4 on v3

--- a/solution.py
+++ b/solution.py
@@ -36,11 +36,21 @@
     return [out[:, k * columns : (k + 1) * columns] for k in range(len(slabs))]
 
 
-def cycle_kernel(gu, gv, grid_at, panel_at, scale, rows, panel, model, minus, plus,
-                 model_next, answer, wide, cross, picked):
+def cycle_kernel(gu, gv, capacity, ids, rows, panel_in, model_in, minus, plus,
+                 model_next, answer, wide, cross, picked, panel, model, sems):
     cells = gu * gv
     slots, columns = rows.shape
     half = columns // 2
+    runs = capacity // 16
+    bits = gu.bit_length() - 1
+    assert gu == gv == 1 << bits
+    panel_copy = pltpu.make_async_copy(panel_in, panel, sems.at[0])
+    model_copy = pltpu.make_async_copy(model_in, model, sems.at[1])
+    panel_copy.start()
+    model_copy.start()
+
+    def grid_at(i, k):
+        return ids[lax.div(i, runs), 0, lax.rem(i, runs) * 16 + k]
 
     chunk = 512
 
@@ -48,15 +58,26 @@
     def _(i):
         at = pl.ds(pl.multiple_of(i * chunk, chunk), chunk)
         wide[at, :] = jnp.zeros((chunk, columns), jnp.float32)
+
+    panel_copy.wait()
+
+    @pl.loop(0, cells // chunk)
+    def _(i):
+        at = pl.ds(pl.multiple_of(i * chunk, chunk), chunk)
         cross[at, :] = panel[at, :].astype(jnp.float32)
 
     wide[pl.ds(cells, 8), :] = jnp.zeros((8, columns), jnp.float32)
 
-    @pl.loop(0, slots // 16)
-    def _(i):
+    def pick(i, used):
         base = pl.multiple_of(i * 16, 16)
         for k in range(16):
-            picked[pl.ds(base + k, 1), :] = cross[pl.ds(panel_at[base + k], 1), :]
+            here = grid_at(i, k)
+            used += (here < cells).astype(jnp.int32)
+            here = jnp.minimum(here, cells - 1)
+            picked[pl.ds(base + k, 1), :] = cross[pl.ds(((here & (gu - 1)) << bits) + (here >> bits), 1), :]
+        return used
+
+    used = lax.fori_loop(0, slots // 16, pick, jnp.int32(0))
 
     lane = lax.broadcasted_iota(jnp.int32, (slots, columns), 1)
     kernel_rows = picked[...]
@@ -70,7 +91,7 @@
     def _(i):
         base = pl.multiple_of(i * 16, 16)
         for k in range(16):
-            at = pl.ds(grid_at[base + k], 1)
+            at = pl.ds(grid_at(i, k), 1)
             wide[at, :] += cross[pl.ds(base + k, 1), :]
 
     @pl.loop(0, gv // GROUP, unroll=UNROLL)
@@ -80,7 +101,9 @@
         for k in range(GROUP):
             cross[pl.ds(GROUP * i + k, gu, stride=gv), :] = out[k]
 
-    gain = scale[0]
+    count = jnp.full((1, columns), used, jnp.int32).astype(jnp.float32)
+    gain = LOOP_GAIN / jnp.sqrt(count)
+    model_copy.wait()
 
     @pl.loop(0, gu // GROUP, unroll=UNROLL)
     def _(i):
@@ -90,12 +113,15 @@
         updated = []
         for k in range(GROUP):
             value = (model[at[k], :].astype(jnp.float32) + gain * out[k]).astype(jnp.bfloat16)
-            model_next[at[k], :] = value
+            model[at[k], :] = value
             updated.append(value.astype(jnp.float32))
         out = stage(plus[...], updated)
         for k in range(GROUP):
             wide[pl.ds(GROUP * i + k, gv, stride=gu), :] = out[k]
 
+    next_copy = pltpu.make_async_copy(model, model_next, sems.at[2])
+    next_copy.start()
+
     @pl.loop(0, gv // GROUP, unroll=UNROLL)
     def _(i):
         base = pl.multiple_of(i * (GROUP * gu), GROUP * gu)
@@ -109,7 +135,7 @@
     def _(i):
         base = pl.multiple_of(i * 16, 16)
         for k in range(16):
-            wide[pl.ds(base + k, 1), :] = cross[pl.ds(grid_at[base + k], 1), :]
+            wide[pl.ds(base + k, 1), :] = cross[pl.ds(grid_at(i, k), 1), :]
 
     kernel_rows = picked[...]
     swapped = pltpu.roll(kernel_rows, half, 1)
@@ -118,28 +144,33 @@
     found = wide[pl.ds(0, slots), :] * (1.0 / math.sqrt(cells))
     predicted = found * real - turned(found) * imag
     answer[...] = (rows[...].astype(jnp.float32) - predicted).astype(jnp.bfloat16)
-
-
-def run_cycle(gu, gv, grid_at, panel_at, scale, rows, panel, model):
+    next_copy.wait()
+
+
+def run_cycle(gu, gv, ids, rows, panel, model):
     cells = gu * gv
     slots, columns = rows.shape
     smem = pl.BlockSpec(memory_space=pltpu.SMEM)
     vmem = pl.BlockSpec(memory_space=pltpu.VMEM)
+    hbm = pl.BlockSpec(memory_space=pl.ANY)
     return pl.pallas_call(
-        functools.partial(cycle_kernel, gu, gv),
+        functools.partial(cycle_kernel, gu, gv, slots // ids.shape[0]),
         out_shape=(
             jax.ShapeDtypeStruct((cells, columns), jnp.bfloat16),
             jax.ShapeDtypeStruct((slots, columns), jnp.bfloat16),
         ),
-        in_specs=[smem] * 3 + [vmem] * 5,
-        out_specs=(vmem, vmem),
+        in_specs=[smem, vmem, hbm, hbm, vmem, vmem],
+        out_specs=(hbm, vmem),
         scratch_shapes=[
             pltpu.VMEM((cells + 8, columns), jnp.float32),
             pltpu.VMEM((cells + 8, columns), jnp.float32),
             pltpu.VMEM((slots, columns), jnp.float32),
+            pltpu.VMEM((cells, columns), jnp.bfloat16),
+            pltpu.VMEM((cells, columns), jnp.bfloat16),
+            pltpu.SemaphoreType.DMA((3,)),
         ],
         compiler_params=pltpu.CompilerParams(vmem_limit_bytes=50 * 1024 * 1024),
-    )(grid_at, panel_at, scale, rows, panel, model, dft_table(gu, -1), dft_table(gu, 1))
+    )(ids, rows, panel, model, dft_table(gu, -1), dft_table(gu, 1))
 
 
 def greet(peers):
@@ -206,39 +237,39 @@
         pltpu.make_async_copy(taper, panel.at[me], own_sems.at[2]),
     ]
 
-    def ring(way, step, peer):
-        if step == 0:
-            source, target = taper, panel.at[me]
-        else:
-            block = owner(-step if way == 0 else step)
-            source = target = panel.at[block]
-            if step == chips // 2 - 1:
-                part = pl.ds(way * half, half)
-                source = target = panel.at[block, part]
-        return sent(source, target, ring_send.at[way, step], ring_recv.at[way, step], peer)
-
-    started = []
-    going = [ring(0, 0, right), ring(1, 0, left)]
+    def goes(way, step, piece):
+        return step < chips // 2 - 1 or (step == chips // 2 - 1 and piece == way)
+
+    def ring(way, step, piece):
+        part = pl.ds(piece * half, half)
+        block = owner(-step if way == 0 else step)
+        source = taper.at[part] if step == 0 else panel.at[block, part]
+        at = (way, step, piece)
+        peer = right if way == 0 else left
+        return sent(source, panel.at[block, part], ring_send.at[at], ring_recv.at[at], peer)
+
+    started = {}
+    for piece in range(2):
+        for way in range(2):
+            started[way, 0, piece] = ring(way, 0, piece)
     moves = swap_blocks(peers, ids, ids_out, id_send, id_recv)
     moves += swap_blocks(peers, rows, rows_out, row_send, row_recv)
-    passed = [sent(taper, panel.at[me], pass_send.at[0, 0], pass_recv.at[0, 0], sibling)]
+    passed = [sent(taper, panel.at[me], pass_send.at[0, 0, 0], pass_recv.at[0, 0, 0], sibling)]
     for copy in own:
         copy.start()
     for step in range(chips // 2):
-        arrived = going
-        started += going
-        going = []
-        for way in range(2):
-            arrived[way].wait_recv()
-            if step + 1 < chips // 2:
-                going.append(ring(way, step + 1, right if way == 0 else left))
-            block = owner(-(step + 1) if way == 0 else step + 1)
-            fresh = panel.at[block]
-            if step == chips // 2 - 1:
-                fresh = panel.at[block, pl.ds(way * half, half)]
-            at = (way, step + 1)
-            passed.append(sent(fresh, fresh, pass_send.at[at], pass_recv.at[at], sibling))
-    for copy in started:
+        for piece in range(2):
+            for way in range(2):
+                if not goes(way, step, piece):
+                    continue
+                started[way, step, piece].wait_recv()
+                if goes(way, step + 1, piece):
+                    started[way, step + 1, piece] = ring(way, step + 1, piece)
+                block = owner(-(step + 1) if way == 0 else step + 1)
+                fresh = panel.at[block, pl.ds(piece * half, half)]
+                at = (way, step + 1, piece)
+                passed.append(sent(fresh, fresh, pass_send.at[at], pass_recv.at[at], sibling))
+    for copy in started.values():
         copy.wait_send()
     for copy in moves + passed:
         copy.wait()
@@ -259,8 +290,8 @@
         ),
         in_specs=[hbm] * 3,
         out_specs=(hbm,) * 3,
-        scratch_shapes=[dma((3,))] + [dma((peers,))] * 4 + [dma((2, steps))] * 2
-        + [dma((2, steps + 1))] * 2,
+        scratch_shapes=[dma((3,))] + [dma((peers,))] * 4 + [dma((2, steps, 2))] * 2
+        + [dma((2, steps + 1, 2))] * 2,
         compiler_params=pltpu.CompilerParams(collective_id=0, has_side_effects=True),
     )(rows, ids, taper)
 
@@ -304,19 +335,14 @@
     send_rows = jnp.dot(
         placed.astype(jnp.bfloat16), visibility, preferred_element_type=jnp.float32
     ).astype(jnp.bfloat16)
-    send_cells = jnp.min(jnp.where(placed, cell_of[None, :], cells), axis=1)
+    turned_cell = cell_of % gv * gu + cell_of // gv
+    send_cells = jnp.min(jnp.where(placed, turned_cell[None, :], cells), axis=1)
 
     ids = jnp.pad(send_cells.reshape(peers, 1, capacity), ((0, 0), (0, 7), (0, 128 - capacity)))
     rows, ids, panel = spread(peers, send_rows.reshape(peers, capacity, columns), ids, taper)
     rows = rows.reshape(slots, columns)
     panel = panel.reshape(cells, columns)
-    cell_ids = ids[:, 0, :capacity].reshape(slots)
-
-    used = cell_ids < cells
-    scale = LOOP_GAIN / jnp.sqrt(jnp.sum(used.astype(jnp.float32)))
-    grid_at = jnp.where(used, cell_ids % gv * gu + cell_ids // gv, cells)
-    panel_at = jnp.minimum(cell_ids, cells - 1)
-    model_next, answer = run_cycle(gu, gv, grid_at, panel_at, scale.reshape(1), rows, panel, model)
+    model_next, answer = run_cycle(gu, gv, ids, rows, panel, model)
 
     returned = send_back(peers, answer.reshape(peers, capacity, columns)).reshape(slots, columns)
     residual = lax.dot_general(

time: 102 us -> 101 us (level)
  Pallas kernels: 87.7 us -> 90.2 us
  other arithmetic: 4.77 us -> 2.63 us
    pallas_call x1, Pallas kernels: 38.4 us -> 43.4 us  [run_cycle(): pl.pallas_call(functools.partial(cycle_kernel, gu, gv, slots // ids.shape...]
    pallas_call x1, Pallas kernels: 40.6 us -> 38.1 us  [spread(): pl.pallas_call(functools.partial(spread_kernel, peers), out_shape=(jax.Sh...]
    reduce_sum x1 -> x0, other arithmetic: 1.46 us -> none  [body(): scale = LOOP_GAIN / jnp.sqrt(jnp.sum(used.astype(jnp.float32)))]
    unnamed x6 -> x8, local copies, waits for them, and re-layouts: 1.65 us -> 2.47 us
where the time goes in v4:
time: 101 us; the launch traced here: 100 us
  Pallas kernels  90.2 us (89%)
  matrix products  3.56 us (4%)
  local copies, waits for them, and re-layouts  3.19 us (3%)
  other arithmetic  2.63 us (3%)
    pallas_call x1, Pallas kernels, run_cycle(): pl.pallas_call(functools.partial(cycle_kernel, gu, gv, slots // ids.shape...  43.4 us
    pallas_call x1, Pallas kernels, spread(): pl.pallas_call(functools.partial(spread_kernel, peers), out_shape=(jax.Sh...  38.1 us
    pallas_call x1, Pallas kernels, send_back(): pl.pallas_call(functools.partial(back_kernel, peers), out_shape=jax.Shape...  8.64 us
    unnamed x8, local copies, waits for them, and re-layouts  2.47 us
    dot_general x1, matrix products, body(): lax.dot_general(placed.astype(jnp.bfloat16), returned, (((0,), (0,)), (()...  2.39 us

profile of v4, /device:TPU:1, one launch (start us, length us, event | category | flops | bytes accessed | tf_op | source)
XLA Modules:
  0.0 100.2 jit_solution(10918040348941488108)
XLA Ops:
  0.6 0.0 copy-start
  0.6 1.0 %convert_reduce_fusion = s32[512]{0:T(512)S(1)} fusion(s32[512]{0:T(512)} %bitcast.13), kind=kLoop, calls=%fused_computation.8 | loop fusion | flops 1310208 | bytes 4096 | tf_op jit(solution)/shard_map/reduce_sum | solution.py:333
  1.7 0.7 fusion.16
  2.4 0.4 select_reduce_fusion
  2.7 0.1 reshape.33
  2.8 0.3 fusion.14
  3.1 0.6 pad.4.ids
  3.7 0.3 multiply_convert_fusion
  4.0 0.0 copy-done
  4.0 1.2 %fusion.2 = bf16[1024,128]{1,0:T(8,128)(2,1)} fusion(bf16[512,128]{1,0:T(8,128)(2,1)S(1)} %copy-done, s32[512]{0:T(512)S(1)} %get-tuple-element.15), kind=kOutput, calls=%fused_computation.4 | convolution fusion | flops 134873088 | bytes 395264 | tf_op jit(solution)/shard_map/dot_general | solution.py:335
  5.2 38.1 %shard_map.68 = (bf16[16,64,128]{2,1,0:T(8,128)(2,1)}, s32[16,8,128]{2,1,0:T(8,128)}, bf16[16,1024,128]{2,1,0:T(8,128)(2,1)}) custom-call(bf16[16,64,128]{2,1,0:T(8,128)(2,1)} %bitcast.11, s32[16,8,128]{2,1,0:T(8,128)} %pad.4.ids, bf16[1024,128]{1,0:T(8,128)(2,1)} %taper.1), custom_call_target="tpu_custom_call" | custom-call | tf_op jit(solution)/shard_map/pallas_call | solution.py:284
  43.3 0.0 copy-start.1
  43.3 0.9 copy-done.1
  44.2 0.0 copy-start.3
  44.3 0.8 copy-done.3
  45.1 43.4 %shard_map.69 = (bf16[16384,128]{1,0:T(8,128)(2,1)}, bf16[1024,128]{1,0:T(8,128)(2,1)S(1)}) custom-call(s32[16,8,128]{2,1,0:T(8,128)S(1)} %copy-done.3, bf16[1024,128]{1,0:T(8,128)(2,1)S(1)} %bitcast.8, bf16[16384,128]{1,0:T(8,128)(2,1)} %bitcast.10, bf16[16384,128]{1,0:T(8,128)(2,1)} %model_in.1, bf16[128,256]{1,0:T(8,128)(2,1)S(1)} %get-tuple-element.13.minus, ...), custom_call_target="tpu_custom_call" | custom-call | tf_op jit(solution)/shard_map/pallas_call | solution.py:156
  88.5 0.0 copy-start.2
  88.5 0.7 copy-done.2
  89.2 8.6 %shard_map.70 = bf16[16,64,128]{2,1,0:T(8,128)(2,1)} custom-call(bf16[16,64,128]{2,1,0:T(8,128)(2,1)} %bitcast.9), custom_call_target="tpu_custom_call" | custom-call | tf_op jit(solution)/shard_map/pallas_call | solution.py:312
  97.9 2.4 %fusion.3 = bf16[512,128]{1,0:T(8,128)(2,1)} fusion(bf16[1024,128]{1,0:T(8,128)(2,1)} %bitcast.12, s32[512]{0:T(512)S(1)} %get-tuple-element.15), kind=kOutput, calls=%fused_computation.5 | convolution fusion | flops 134807552 | bytes 395264 | tf_op jit(solution)/shard_map/dot_general | solution.py:348
  (1 shorter events, 0.0 us)
Async XLA Ops:
  0.6 3.4 %copy-start = (bf16[512,128]{1,0:T(8,128)(2,1)S(1)}, bf16[512,128]{1,0:T(8,128)(2,1)}, u32[]{:S(2)}) copy-start(bf16[512,128]{1,0:T(8,128)(2,1)} %param.5) | copy-start | bytes 393220
  43.3 1.0 copy-start.1
  44.2 0.8 copy-start.3
  88.5 0.7 copy-start.2

commit v5 on v4

--- a/solution.py
+++ b/solution.py
@@ -10,8 +10,9 @@
 
 LOOP_GAIN = 0.1
 MESH = pl.DeviceIdType.MESH
-GROUP = 8
+GROUP = 16
 UNROLL = 2
+PAD = 8
 
 
 def dft_table(length, orient):
@@ -99,7 +100,7 @@
         base = pl.multiple_of(i * (GROUP * gu), GROUP * gu)
         out = stage(minus[...], [wide[pl.ds(base + k * gu, gu), :] for k in range(GROUP)])
         for k in range(GROUP):
-            cross[pl.ds(GROUP * i + k, gu, stride=gv), :] = out[k]
+            cross[pl.ds(GROUP * i + k, gu, stride=gv + PAD), :] = out[k]
 
     count = jnp.full((1, columns), used, jnp.int32).astype(jnp.float32)
     gain = LOOP_GAIN / jnp.sqrt(count)
@@ -109,7 +110,8 @@
     def _(i):
         base = pl.multiple_of(i * (GROUP * gv), GROUP * gv)
         at = [pl.ds(base + k * gv, gv) for k in range(GROUP)]
-        out = stage(minus[...], [cross[here, :] for here in at])
+        apart = pl.multiple_of(i * (GROUP * (gv + PAD)), 8)
+        out = stage(minus[...], [cross[pl.ds(apart + k * (gv + PAD), gv), :] for k in range(GROUP)])
         updated = []
         for k in range(GROUP):
             value = (model[at[k], :].astype(jnp.float32) + gain * out[k]).astype(jnp.bfloat16)
@@ -117,7 +119,7 @@
             updated.append(value.astype(jnp.float32))
         out = stage(plus[...], updated)
         for k in range(GROUP):
-            wide[pl.ds(GROUP * i + k, gv, stride=gu), :] = out[k]
+            wide[pl.ds(GROUP * i + k, gv, stride=gu + PAD), :] = out[k]
 
     next_copy = pltpu.make_async_copy(model, model_next, sems.at[2])
     next_copy.start()
@@ -125,7 +127,8 @@
     @pl.loop(0, gv // GROUP, unroll=UNROLL)
     def _(i):
         base = pl.multiple_of(i * (GROUP * gu), GROUP * gu)
-        out = stage(plus[...], [wide[pl.ds(base + k * gu, gu), :] for k in range(GROUP)])
+        apart = pl.multiple_of(i * (GROUP * (gu + PAD)), 8)
+        out = stage(plus[...], [wide[pl.ds(apart + k * (gu + PAD), gu), :] for k in range(GROUP)])
         for k in range(GROUP):
             cross[pl.ds(base + k * gu, gu), :] = out[k]
 
@@ -162,8 +165,8 @@
         in_specs=[smem, vmem, hbm, hbm, vmem, vmem],
         out_specs=(hbm, vmem),
         scratch_shapes=[
-            pltpu.VMEM((cells + 8, columns), jnp.float32),
-            pltpu.VMEM((cells + 8, columns), jnp.float32),
+            pltpu.VMEM((gv * (gu + PAD) + 8, columns), jnp.float32),
+            pltpu.VMEM((gu * (gv + PAD) + 8, columns), jnp.float32),
             pltpu.VMEM((slots, columns), jnp.float32),
             pltpu.VMEM((cells, columns), jnp.bfloat16),
             pltpu.VMEM((cells, columns), jnp.bfloat16),
@@ -338,7 +341,7 @@
     turned_cell = cell_of % gv * gu + cell_of // gv
     send_cells = jnp.min(jnp.where(placed, turned_cell[None, :], cells), axis=1)
 
-    ids = jnp.pad(send_cells.reshape(peers, 1, capacity), ((0, 0), (0, 7), (0, 128 - capacity)))
+    ids = jnp.pad(send_cells.reshape(peers, 1, capacity), ((0, 0), (0, 0), (0, 128 - capacity)))
     rows, ids, panel = spread(peers, send_rows.reshape(peers, capacity, columns), ids, taper)
     rows = rows.reshape(slots, columns)
     panel = panel.reshape(cells, columns)

time: 101 us -> 87.3 us (0.86)
  Pallas kernels: 90.2 us -> 76.9 us
    pallas_call x1, Pallas kernels: 43.4 us -> 30.9 us  [run_cycle(): pl.pallas_call(functools.partial(cycle_kernel, gu, gv, slots // ids.shape...]
    pallas_call x1, Pallas kernels: 38.1 us -> 36.9 us  [spread(): pl.pallas_call(functools.partial(spread_kernel, peers), out_shape=(jax.Sh...]
where the time goes in v5:
time: 87.3 us; the launch traced here: 86.8 us
  Pallas kernels  76.9 us (88%)
  matrix products  3.55 us (4%)
  local copies, waits for them, and re-layouts  3.02 us (3%)
  other arithmetic  2.63 us (3%)
    pallas_call x1, Pallas kernels, spread(): pl.pallas_call(functools.partial(spread_kernel, peers), out_shape=(jax.Sh...  36.9 us
    pallas_call x1, Pallas kernels, run_cycle(): pl.pallas_call(functools.partial(cycle_kernel, gu, gv, slots // ids.shape...  30.9 us
    pallas_call x1, Pallas kernels, send_back(): pl.pallas_call(functools.partial(back_kernel, peers), out_shape=jax.Shape...  9.17 us
    dot_general x1, matrix products, body(): lax.dot_general(placed.astype(jnp.bfloat16), returned, (((0,), (0,)), (()...  2.38 us
    unnamed x8, local copies, waits for them, and re-layouts  2.33 us

profile of v5, /device:TPU:1, one launch (start us, length us, event | category | flops | bytes accessed | tf_op | source)
XLA Modules:
  0.0 86.8 jit_solution(9564869986923513213)
XLA Ops:
  0.6 0.0 copy-start
  0.6 1.0 %convert_reduce_fusion = s32[512]{0:T(512)S(1)} fusion(s32[512]{0:T(512)} %bitcast.13), kind=kLoop, calls=%fused_computation.8 | loop fusion | flops 1310208 | bytes 4096 | tf_op jit(solution)/shard_map/reduce_sum | solution.py:336
  1.7 0.7 fusion.16
  2.4 0.4 select_reduce_fusion
  2.7 0.1 reshape.33
  2.8 0.6 pad.4.ids
  3.4 0.3 fusion.14
  3.7 0.3 multiply_convert_fusion
  4.0 0.0 copy-done
  4.0 1.2 %fusion.2 = bf16[1024,128]{1,0:T(8,128)(2,1)} fusion(bf16[512,128]{1,0:T(8,128)(2,1)S(1)} %copy-done, s32[512]{0:T(512)S(1)} %get-tuple-element.15), kind=kOutput, calls=%fused_computation.4 | convolution fusion | flops 134873088 | bytes 395264 | tf_op jit(solution)/shard_map/dot_general | solution.py:338
  5.2 36.9 %shard_map.68 = (bf16[16,64,128]{2,1,0:T(8,128)(2,1)}, s32[16,1,128]{2,1,0:T(1,128)}, bf16[16,1024,128]{2,1,0:T(8,128)(2,1)}) custom-call(bf16[16,64,128]{2,1,0:T(8,128)(2,1)} %bitcast.11, s32[16,1,128]{2,1,0:T(1,128)} %pad.4.ids, bf16[1024,128]{1,0:T(8,128)(2,1)} %taper.1), custom_call_target="tpu_custom_call" | custom-call | tf_op jit(solution)/shard_map/pallas_call | solution.py:287
  42.0 0.0 copy-start.1
  42.1 0.9 %copy-done.1 = bf16[16,64,128]{2,1,0:T(8,128)(2,1)S(1)} copy-done((bf16[16,64,128]{2,1,0:T(8,128)(2,1)S(1)}, bf16[16,64,128]{2,1,0:T(8,128)(2,1)}, u32[]{:S(2)}) %copy-start.1) | copy-done | bytes 262168
  43.0 0.0 copy-start.3
  43.0 0.7 copy-done.3
  43.7 30.9 %shard_map.69 = (bf16[16384,128]{1,0:T(8,128)(2,1)}, bf16[1024,128]{1,0:T(8,128)(2,1)S(1)}) custom-call(s32[16,1,128]{2,1,0:T(1,128)S(1)} %copy-done.3, bf16[1024,128]{1,0:T(8,128)(2,1)S(1)} %bitcast.8, bf16[16384,128]{1,0:T(8,128)(2,1)} %bitcast.10, bf16[16384,128]{1,0:T(8,128)(2,1)} %model_in.1, bf16[128,256]{1,0:T(8,128)(2,1)S(1)} %get-tuple-element.13.minus, ...), custom_call_target="tpu_custom_call" | custom-call | tf_op jit(solution)/shard_map/pallas_call | solution.py:159
  74.6 0.0 copy-start.2
  74.6 0.7 copy-done.2
  75.3 9.2 %shard_map.70 = bf16[16,64,128]{2,1,0:T(8,128)(2,1)} custom-call(bf16[16,64,128]{2,1,0:T(8,128)(2,1)} %bitcast.9), custom_call_target="tpu_custom_call" | custom-call | tf_op jit(solution)/shard_map/pallas_call | solution.py:315
  84.5 2.4 %fusion.3 = bf16[512,128]{1,0:T(8,128)(2,1)} fusion(bf16[1024,128]{1,0:T(8,128)(2,1)} %bitcast.12, s32[512]{0:T(512)S(1)} %get-tuple-element.15), kind=kOutput, calls=%fused_computation.5 | convolution fusion | flops 134807552 | bytes 395264 | tf_op jit(solution)/shard_map/dot_general | solution.py:351
  (1 shorter events, 0.0 us)
Async XLA Ops:
  0.6 3.4 %copy-start = (bf16[512,128]{1,0:T(8,128)(2,1)S(1)}, bf16[512,128]{1,0:T(8,128)(2,1)}, u32[]{:S(2)}) copy-start(bf16[512,128]{1,0:T(8,128)(2,1)} %param.5) | copy-start | bytes 393220
  42.0 1.0 %copy-start.1 = (bf16[16,64,128]{2,1,0:T(8,128)(2,1)S(1)}, bf16[16,64,128]{2,1,0:T(8,128)(2,1)}, u32[]{:S(2)}) copy-start(bf16[16,64,128]{2,1,0:T(8,128)(2,1)} %get-tuple-element.8) | copy-start | bytes 786436
  43.0 0.7 copy-start.3
  74.6 0.7 copy-start.2

commit v6 on v5

--- a/solution.py
+++ b/solution.py
@@ -11,7 +11,7 @@
 LOOP_GAIN = 0.1
 MESH = pl.DeviceIdType.MESH
 GROUP = 16
-UNROLL = 2
+UNROLL = 4
 PAD = 8
 
 
@@ -31,8 +31,9 @@
 
 def stage(table, slabs):
     columns = slabs[0].shape[1]
-    top = jnp.concatenate(slabs, 1).astype(jnp.bfloat16)
-    low = jnp.concatenate([turned(slab) for slab in slabs], 1).astype(jnp.bfloat16)
+    slabs = [slab.astype(jnp.bfloat16) for slab in slabs]
+    top = jnp.concatenate(slabs, 1)
+    low = jnp.concatenate([turned(slab) for slab in slabs], 1)
     out = jnp.dot(table, jnp.concatenate([top, low], 0), preferred_element_type=jnp.float32)
     return [out[:, k * columns : (k + 1) * columns] for k in range(len(slabs))]
 
@@ -116,7 +117,7 @@
         for k in range(GROUP):
             value = (model[at[k], :].astype(jnp.float32) + gain * out[k]).astype(jnp.bfloat16)
             model[at[k], :] = value
-            updated.append(value.astype(jnp.float32))
+            updated.append(value)
         out = stage(plus[...], updated)
         for k in range(GROUP):
             wide[pl.ds(GROUP * i + k, gv, stride=gu + PAD), :] = out[k]

time: 87.3 us -> 82.2 us (0.942)
  Pallas kernels: 76.9 us -> 71.9 us
    pallas_call x1, Pallas kernels: 30.9 us -> 25.8 us  [run_cycle(): pl.pallas_call(functools.partial(cycle_kernel, gu, gv, slots // ids.shape...]
where the time goes in v6:
time: 82.2 us; the launch traced here: 81.8 us
  Pallas kernels  71.9 us (87%)
  matrix products  3.55 us (4%)
  local copies, waits for them, and re-layouts  3.02 us (4%)
  other arithmetic  2.63 us (3%)
    pallas_call x1, Pallas kernels, spread(): pl.pallas_call(functools.partial(spread_kernel, peers), out_shape=(jax.Sh...  36.9 us
    pallas_call x1, Pallas kernels, run_cycle(): pl.pallas_call(functools.partial(cycle_kernel, gu, gv, slots // ids.shape...  25.8 us
    pallas_call x1, Pallas kernels, send_back(): pl.pallas_call(functools.partial(back_kernel, peers), out_shape=jax.Shape...  9.2 us
    dot_general x1, matrix products, body(): lax.dot_general(placed.astype(jnp.bfloat16), returned, (((0,), (0,)), (()...  2.38 us
    unnamed x8, local copies, waits for them, and re-layouts  2.33 us

profile of v6, /device:TPU:1, one launch (start us, length us, event | category | flops | bytes accessed | tf_op | source)
XLA Modules:
  0.0 81.8 jit_solution(15906817252807581820)
XLA Ops:
  0.6 0.0 copy-start
  0.6 1.0 %convert_reduce_fusion = s32[512]{0:T(512)S(1)} fusion(s32[512]{0:T(512)} %bitcast.13), kind=kLoop, calls=%fused_computation.8 | loop fusion | flops 1310208 | bytes 4096 | tf_op jit(solution)/shard_map/reduce_sum | solution.py:337
  1.7 0.7 fusion.16
  2.4 0.4 select_reduce_fusion
  2.7 0.1 reshape.33
  2.8 0.6 pad.4.ids
  3.4 0.3 fusion.14
  3.7 0.3 multiply_convert_fusion
  4.0 0.0 copy-done
  4.0 1.2 %fusion.2 = bf16[1024,128]{1,0:T(8,128)(2,1)} fusion(bf16[512,128]{1,0:T(8,128)(2,1)S(1)} %copy-done, s32[512]{0:T(512)S(1)} %get-tuple-element.15), kind=kOutput, calls=%fused_computation.4 | convolution fusion | flops 134873088 | bytes 395264 | tf_op jit(solution)/shard_map/dot_general | solution.py:339
  5.2 36.9 %shard_map.68 = (bf16[16,64,128]{2,1,0:T(8,128)(2,1)}, s32[16,1,128]{2,1,0:T(1,128)}, bf16[16,1024,128]{2,1,0:T(8,128)(2,1)}) custom-call(bf16[16,64,128]{2,1,0:T(8,128)(2,1)} %bitcast.11, s32[16,1,128]{2,1,0:T(1,128)} %pad.4.ids, bf16[1024,128]{1,0:T(8,128)(2,1)} %taper.1), custom_call_target="tpu_custom_call" | custom-call | tf_op jit(solution)/shard_map/pallas_call | solution.py:288
  42.0 0.0 copy-start.1
  42.1 0.9 %copy-done.1 = bf16[16,64,128]{2,1,0:T(8,128)(2,1)S(1)} copy-done((bf16[16,64,128]{2,1,0:T(8,128)(2,1)S(1)}, bf16[16,64,128]{2,1,0:T(8,128)(2,1)}, u32[]{:S(2)}) %copy-start.1) | copy-done | bytes 262168
  43.0 0.0 copy-start.3
  43.0 0.7 copy-done.3
  43.7 25.8 %shard_map.69 = (bf16[16384,128]{1,0:T(8,128)(2,1)}, bf16[1024,128]{1,0:T(8,128)(2,1)S(1)}) custom-call(s32[16,1,128]{2,1,0:T(1,128)S(1)} %copy-done.3, bf16[1024,128]{1,0:T(8,128)(2,1)S(1)} %bitcast.8, bf16[16384,128]{1,0:T(8,128)(2,1)} %bitcast.10, bf16[16384,128]{1,0:T(8,128)(2,1)} %model_in.1, bf16[128,256]{1,0:T(8,128)(2,1)S(1)} %get-tuple-element.13.minus, ...), custom_call_target="tpu_custom_call" | custom-call | tf_op jit(solution)/shard_map/pallas_call | solution.py:160
  69.5 0.0 copy-start.2
  69.5 0.7 copy-done.2
  70.2 9.2 %shard_map.70 = bf16[16,64,128]{2,1,0:T(8,128)(2,1)} custom-call(bf16[16,64,128]{2,1,0:T(8,128)(2,1)} %bitcast.9), custom_call_target="tpu_custom_call" | custom-call | tf_op jit(solution)/shard_map/pallas_call | solution.py:316
  79.4 2.4 %fusion.3 = bf16[512,128]{1,0:T(8,128)(2,1)} fusion(bf16[1024,128]{1,0:T(8,128)(2,1)} %bitcast.12, s32[512]{0:T(512)S(1)} %get-tuple-element.15), kind=kOutput, calls=%fused_computation.5 | convolution fusion | flops 134807552 | bytes 395264 | tf_op jit(solution)/shard_map/dot_general | solution.py:352
  (1 shorter events, 0.0 us)
Async XLA Ops:
  0.6 3.4 %copy-start = (bf16[512,128]{1,0:T(8,128)(2,1)S(1)}, bf16[512,128]{1,0:T(8,128)(2,1)}, u32[]{:S(2)}) copy-start(bf16[512,128]{1,0:T(8,128)(2,1)} %param.5) | copy-start | bytes 393220
  42.0 1.0 %copy-start.1 = (bf16[16,64,128]{2,1,0:T(8,128)(2,1)S(1)}, bf16[16,64,128]{2,1,0:T(8,128)(2,1)}, u32[]{:S(2)}) copy-start(bf16[16,64,128]{2,1,0:T(8,128)(2,1)} %get-tuple-element.8) | copy-start | bytes 786436
  43.0 0.7 copy-start.3
  69.5 0.7 copy-start.2

commit v7 on v6

--- a/solution.py
+++ b/solution.py
@@ -11,7 +11,7 @@
 LOOP_GAIN = 0.1
 MESH = pl.DeviceIdType.MESH
 GROUP = 16
-UNROLL = 4
+UNROLL = 8
 PAD = 8
 
 
@@ -233,13 +233,15 @@
         return chip_at(lax.rem(place + distance + chips, chips), chips) * 2 + core
 
     right, left = owner(1), owner(-1)
-    greet(peers)
 
     own = [
         pltpu.make_async_copy(rows.at[me], rows_out.at[me], own_sems.at[0]),
         pltpu.make_async_copy(ids.at[me], ids_out.at[me], own_sems.at[1]),
         pltpu.make_async_copy(taper, panel.at[me], own_sems.at[2]),
     ]
+    for copy in own:
+        copy.start()
+    greet(peers)
 
     def goes(way, step, piece):
         return step < chips // 2 - 1 or (step == chips // 2 - 1 and piece == way)
@@ -259,8 +261,6 @@
     moves = swap_blocks(peers, ids, ids_out, id_send, id_recv)
     moves += swap_blocks(peers, rows, rows_out, row_send, row_recv)
     passed = [sent(taper, panel.at[me], pass_send.at[0, 0, 0], pass_recv.at[0, 0, 0], sibling)]
-    for copy in own:
-        copy.start()
     for step in range(chips // 2):
         for piece in range(2):
             for way in range(2):

time: 82.2 us -> 81.6 us (level)
    pallas_call x1, Pallas kernels: 25.8 us -> 23.6 us  [run_cycle(): pl.pallas_call(functools.partial(cycle_kernel, gu, gv, slots // ids.shape...]
    pallas_call x1, Pallas kernels: 9.2 us -> 11 us  [send_back(): pl.pallas_call(functools.partial(back_kernel, peers), out_shape=jax.Shape...]
where the time goes in v7:
time: 81.6 us; the launch traced here: 81.3 us
  Pallas kernels  71.4 us (88%)
  matrix products  3.55 us (4%)
  local copies, waits for them, and re-layouts  3.02 us (4%)
  other arithmetic  2.63 us (3%)
    pallas_call x1, Pallas kernels, spread(): pl.pallas_call(functools.partial(spread_kernel, peers), out_shape=(jax.Sh...  36.9 us
    pallas_call x1, Pallas kernels, run_cycle(): pl.pallas_call(functools.partial(cycle_kernel, gu, gv, slots // ids.shape...  23.6 us
    pallas_call x1, Pallas kernels, send_back(): pl.pallas_call(functools.partial(back_kernel, peers), out_shape=jax.Shape...  11 us
    dot_general x1, matrix products, body(): lax.dot_general(placed.astype(jnp.bfloat16), returned, (((0,), (0,)), (()...  2.38 us
    unnamed x8, local copies, waits for them, and re-layouts  2.33 us

profile of v7, /device:TPU:1, one launch (start us, length us, event | category | flops | bytes accessed | tf_op | source)
XLA Modules:
  0.0 81.3 jit_solution(629185886096357109)
XLA Ops:
  0.6 0.0 copy-start
  0.6 1.0 %convert_reduce_fusion = s32[512]{0:T(512)S(1)} fusion(s32[512]{0:T(512)} %bitcast.13), kind=kLoop, calls=%fused_computation.8 | loop fusion | flops 1310208 | bytes 4096 | tf_op jit(solution)/shard_map/reduce_sum | solution.py:337
  1.7 0.7 fusion.16
  2.4 0.4 select_reduce_fusion
  2.7 0.1 reshape.33
  2.8 0.6 pad.4.ids
  3.4 0.3 fusion.14
  3.7 0.3 multiply_convert_fusion
  4.0 0.0 copy-done
  4.0 1.2 %fusion.2 = bf16[1024,128]{1,0:T(8,128)(2,1)} fusion(bf16[512,128]{1,0:T(8,128)(2,1)S(1)} %copy-done, s32[512]{0:T(512)S(1)} %get-tuple-element.15), kind=kOutput, calls=%fused_computation.4 | convolution fusion | flops 134873088 | bytes 395264 | tf_op jit(solution)/shard_map/dot_general | solution.py:339
  5.2 36.9 %shard_map.68 = (bf16[16,64,128]{2,1,0:T(8,128)(2,1)}, s32[16,1,128]{2,1,0:T(1,128)}, bf16[16,1024,128]{2,1,0:T(8,128)(2,1)}) custom-call(bf16[16,64,128]{2,1,0:T(8,128)(2,1)} %bitcast.11, s32[16,1,128]{2,1,0:T(1,128)} %pad.4.ids, bf16[1024,128]{1,0:T(8,128)(2,1)} %taper.1), custom_call_target="tpu_custom_call" | custom-call | tf_op jit(solution)/shard_map/pallas_call | solution.py:288
  42.0 0.0 copy-start.1
  42.1 0.9 %copy-done.1 = bf16[16,64,128]{2,1,0:T(8,128)(2,1)S(1)} copy-done((bf16[16,64,128]{2,1,0:T(8,128)(2,1)S(1)}, bf16[16,64,128]{2,1,0:T(8,128)(2,1)}, u32[]{:S(2)}) %copy-start.1) | copy-done | bytes 262168
  43.0 0.0 copy-start.3
  43.0 0.7 copy-done.3
  43.7 23.6 %shard_map.69 = (bf16[16384,128]{1,0:T(8,128)(2,1)}, bf16[1024,128]{1,0:T(8,128)(2,1)S(1)}) custom-call(s32[16,1,128]{2,1,0:T(1,128)S(1)} %copy-done.3, bf16[1024,128]{1,0:T(8,128)(2,1)S(1)} %bitcast.8, bf16[16384,128]{1,0:T(8,128)(2,1)} %bitcast.10, bf16[16384,128]{1,0:T(8,128)(2,1)} %model_in.1, bf16[128,256]{1,0:T(8,128)(2,1)S(1)} %get-tuple-element.13.minus, ...), custom_call_target="tpu_custom_call" | custom-call | tf_op jit(solution)/shard_map/pallas_call | solution.py:160
  67.3 0.0 copy-start.2
  67.3 0.7 copy-done.2
  68.0 11.0 %shard_map.70 = bf16[16,64,128]{2,1,0:T(8,128)(2,1)} custom-call(bf16[16,64,128]{2,1,0:T(8,128)(2,1)} %bitcast.9), custom_call_target="tpu_custom_call" | custom-call | tf_op jit(solution)/shard_map/pallas_call | solution.py:316
  79.0 2.4 %fusion.3 = bf16[512,128]{1,0:T(8,128)(2,1)} fusion(bf16[1024,128]{1,0:T(8,128)(2,1)} %bitcast.12, s32[512]{0:T(512)S(1)} %get-tuple-element.15), kind=kOutput, calls=%fused_computation.5 | convolution fusion | flops 134807552 | bytes 395264 | tf_op jit(solution)/shard_map/dot_general | solution.py:352
  (1 shorter events, 0.0 us)
Async XLA Ops:
  0.6 3.4 %copy-start = (bf16[512,128]{1,0:T(8,128)(2,1)S(1)}, bf16[512,128]{1,0:T(8,128)(2,1)}, u32[]{:S(2)}) copy-start(bf16[512,128]{1,0:T(8,128)(2,1)} %param.5) | copy-start | bytes 393220
  42.0 1.0 %copy-start.1 = (bf16[16,64,128]{2,1,0:T(8,128)(2,1)S(1)}, bf16[16,64,128]{2,1,0:T(8,128)(2,1)}, u32[]{:S(2)}) copy-start(bf16[16,64,128]{2,1,0:T(8,128)(2,1)} %get-tuple-element.8) | copy-start | bytes 786436
  43.0 0.7 copy-start.3
  67.3 0.7 copy-start.2
